TPU v7x, 512 devices: a whole 4x8x8 slice. The times are simulated.
512 devices in a mesh: dom: 64 (over y, x, core), slab: 8 (over z).
Axes of the slice: x: 4, y: 8, z: 8, core: 2. Of those that a mesh axis runs over, the one named last changes fastest.
Arguments:
- reference_volume: bfloat16 [4096, 128], P('slab'), may hold values from -6 to 6
- cell_index: int32 [128, 3, 64], P('dom'), may hold values from 0 to 4031
- cell_frac: float32 [128, 3, 64], P('dom'), may hold values from 0 to 1
- warp: bfloat16 [4, 128, 3], P(None, 'dom'), may hold values from 0.5 to 2
- series: int32 [16384], P('dom'), may hold values from 0 to 127, as said below
- position: float32 [16384], P('dom'), may hold values from 0 to 1
- images: bfloat16 [16384, 3, 64, 128], P('dom', None, 'slab'), may hold values from -6 to 6
Outputs:
- residual: bfloat16 [16384, 3, 64, 128], P('dom', None, 'slab')
- warp_grad: float32 [4, 128, 3], P(None, 'dom')
- back_volume: float32 [4096, 128], P('slab')
Inputs may be any that keep to these rules, and one draw needn't show every extreme that they name: Every series has at least one particle; series differ in their expected share of particles by up to three-fold.
All inputs are finite; a program needn't handle non-finite values.
Results may differ from a plain program's by a relative error of at most 0.0055.
Values may be sent and summed in bfloat16 or wider, within the bound.
A program may use at most 64 MiB of HBM per device.

v0:
```python
import jax
import jax.numpy as jnp
from jax import lax
from jax.sharding import PartitionSpec as P

HIGHEST_MODE = lax.Precision.HIGHEST


def bspline_basis(location):
    remain = 1.0 - location
    square = location * location
    cubed = square * location
    return jnp.stack(
        [
            remain * remain * remain / 6.0,
            (3.0 * cubed - 6.0 * square + 4.0) / 6.0,
            (-3.0 * cubed + 3.0 * square + 3.0 * location + 1.0) / 6.0,
            cubed / 6.0,
        ],
        axis=1,
    )


def cell_weights(lower_cell, fraction, cell_ids, plane_size):
    lower_part = jnp.where(cell_ids == lower_cell[..., None], 1.0 - fraction[..., None], 0.0)
    upper_part = jnp.where(cell_ids == lower_cell[..., None] + plane_size, fraction[..., None], 0.0)
    return lower_part + upper_part


def spread_cells(lower_cell, fraction, back_rows, first, row_count, plane_size):
    columns = back_rows.shape[3]
    flat_low = jnp.transpose(lower_cell, (2, 0, 1)).reshape(-1)
    flat_frac = jnp.transpose(fraction, (2, 0, 1)).reshape(-1)
    values = back_rows.reshape(-1, columns)

    def place(cells, share):
        offset = cells - first
        offset = jnp.where((offset >= 0) & (offset < row_count), offset, row_count)
        target = jnp.zeros((row_count, columns), jnp.float32)
        return target.at[offset].add(share[:, None] * values, mode="drop")

    return place(flat_low, 1.0 - flat_frac) + place(flat_low + plane_size, flat_frac)


def shards(reference_volume, cell_index, cell_frac, warp, series, position, images):
    slab_rows = reference_volume.shape[0]
    slab_count = lax.axis_size("slab")
    slab_place = lax.axis_index("slab")
    plane_size = cell_index.shape[2]
    band_rows = plane_size // slab_count
    volume = reference_volume.astype(jnp.float32)
    own_cells = slab_place * slab_rows + jnp.arange(slab_rows, dtype=jnp.int32)
    weights = cell_weights(cell_index, cell_frac, own_cells, plane_size)
    projected = lax.psum_scatter(
        jnp.einsum("stuc,cx->ustx", weights, volume, precision=HIGHEST_MODE).astype(jnp.bfloat16),
        "slab",
        scatter_dimension=0,
        tiled=True,
    )
    proj_piece = lax.all_gather(projected, "dom", axis=1, tiled=True)
    warp_piece = lax.all_gather(warp, "dom", axis=1, tiled=True)
    series_ids = jnp.arange(proj_piece.shape[1], dtype=jnp.int32)
    picked = (series[:, None] == series_ids[None, :]).astype(jnp.bfloat16)
    predicted = jnp.einsum("pj,ujtx->ptux", picked, proj_piece, preferred_element_type=jnp.float32)
    chosen = jnp.einsum("pj,cjt->ptc", picked, warp_piece, preferred_element_type=jnp.float32)
    predicted, chosen = (predicted, chosen)
    spline_basis = bspline_basis(position)
    tilt_scale = jnp.einsum("pc,ptc->pt", spline_basis, chosen, precision=HIGHEST_MODE)
    residual = (images.astype(jnp.float32) - tilt_scale[:, :, None, None] * predicted).astype(
        jnp.bfloat16
    )
    rounded = lax.optimization_barrier(residual).astype(jnp.float32)
    inner_sum = jnp.sum(rounded * predicted, axis=(2, 3))
    total_series = warp.shape[1] * lax.axis_size("dom")
    member = (series[:, None] == jnp.arange(total_series, dtype=jnp.int32)[None, :]).astype(
        jnp.float32
    )
    weighted = tilt_scale[:, :, None, None] * rounded
    series_back = jnp.einsum("pm,ptux->umtx", member, weighted, precision=HIGHEST_MODE)
    warp_part = jnp.einsum(
        "pm,pc,pt->cmt", member, spline_basis, inner_sum, precision=HIGHEST_MODE
    ) * (-1.0 / (plane_size * plane_size))
    band_first = slab_place * band_rows
    back_rows, own_warp = (
        lax.psum_scatter(series_back, "dom", scatter_dimension=1, tiled=True),
        lax.psum_scatter(warp_part, "dom", scatter_dimension=1, tiled=True),
    )
    table_cells, table_frac = (cell_index, cell_frac)
    warp_grad = lax.psum(own_warp, "slab")
    band_cells = lax.dynamic_slice_in_dim(table_cells, band_first, band_rows, 2)
    band_frac = lax.dynamic_slice_in_dim(table_frac, band_first, band_rows, 2)
    spread = spread_cells(band_cells, band_frac, back_rows, 0, plane_size * plane_size, plane_size)
    summed = lax.psum(spread, ("dom", "slab"))
    back_volume = lax.dynamic_slice_in_dim(summed, slab_place * slab_rows, slab_rows, 0)
    return (residual, warp_grad, back_volume)


def solution(mesh):
    placed = (
        P("slab", None),
        P("dom", None, None),
        P("dom", None, None),
        P(None, "dom", None),
        P("dom"),
        P("dom"),
        P("dom", None, "slab", None),
    )
    return jax.shard_map(
        shards,
        mesh=mesh,
        in_specs=placed,
        out_specs=(P("dom", None, "slab", None), P(None, "dom", None), P("slab", None)),
        check_vma=False,
    )
```

profile of v0, /device:TPU:1, one launch (start us, length us, event | category | flops | bytes accessed | tf_op | source)
XLA Modules:
  0.0 586.9 jit_solution(15047955221191717650)
XLA Ops:
  7.2 0.0 copy-start
  7.2 0.0 all-reduce.8.cloned.1.call-start
  7.2 0.8 broadcast_add_fusion
  8.0 0.7 copy.34
  8.7 0.7 broadcast_subtract_fusion
  9.4 0.7 copy.37
  10.1 0.7 fusion.8
  10.8 0.7 copy.38
  11.5 0.0 all-reduce.8.cloned.1.call-update
  11.6 0.0 reduce-scatter.4.cloned.1.call-start
  11.6 0.7 fusion.49
  12.3 0.8 copy.32
  13.1 53.1 %all_gather.6 = bf16[4,128,3]{2,0,1:T(4,128)(2,1)S(1)} all-gather(bf16[4,2,3]{2,0,1:T(4,128)(2,1)S(1)} %copy.32), channel_id=1, replica_groups=mesh['dom'=64,'slab'=8] {'dom'}, dimensions={1}, use_global_device_ids=true | all-gather | bytes 3120 | tf_op jit(solution)/shard_map/all_gather | solution.py:61
  66.2 1.0 copy.33
  67.1 1.2 copy.31
  68.3 1.3 dynamic-slice
  70.3 0.2 fusion.9
  70.5 19.8 %all-reduce.8.cloned.1.call-done = bf16[64,2,3,128]{3,1,2,0:T(2,128)(2,1)} async-done(((bf16[64,2,3,128]{3,1,2,0:T(2,128)(2,1)}), bf16[64,2,3,128]{3,1,2,0:T(2,128)(2,1)}) %all-reduce.8.cloned.1.call-update) | async-done | bytes 98320
  90.3 0.7 constant_dynamic-slice_fusion.1
  91.1 56.0 %all_gather.7 = bf16[8,128,3,128]{3,0,2,1:T(8,128)(2,1)S(1)} all-gather(bf16[8,2,3,128]{3,0,2,1:T(8,128)(2,1)S(1)} %copy.39), channel_id=1, replica_groups=mesh['dom'=64,'slab'=8] {'dom'}, dimensions={1}, use_global_device_ids=true | all-gather | bytes 798720 | tf_op jit(solution)/shard_map/all_gather | solution.py:60
  147.1 0.7 fusion.2
  147.8 0.6 convert_multiply_fusion
  148.4 1.6 fusion.5
  150.0 0.0 copy-start.2
  150.0 1.6 copy.45
  151.7 0.0 reduce-scatter.4.cloned.1.call-update
  151.7 0.0 all-reduce.6.cloned.1.call-start
  151.7 0.1 dynamic-slice_bitcast_fusion
  151.8 0.1 copy.43
  151.9 0.1 reshape.105
  152.0 0.1 dynamic-slice_bitcast_fusion.1
  152.1 0.1 copy.42
  152.2 0.1 reshape.104
  152.3 0.1 add_bitcast_fusion
  152.4 137.1 %reduce-scatter.4.cloned.1.call-done = f32[8,2,3,128]{3,0,2,1:T(8,128)} async-done(((f32[8,128,3,128]{3,0,2,1:T(8,128)}), f32[8,2,3,128]{3,0,2,1:T(8,128)}) %reduce-scatter.4.cloned.1.call-update) | async-done | bytes 24592
  289.5 0.7 copy.46
  290.3 0.1 broadcast_multiply_fusion.1
  290.4 2.3 scatter_custom_fusion
  292.7 0.0 all-reduce.6.cloned.1.call-update
  292.7 1.3 dynamic-slice.2
  294.6 1.9 copy.47
  296.5 0.2 fusion.10
  296.7 0.2 copy.41
  296.9 246.5 %all-reduce.1 = f32[4,128,3]{2,0,1:T(4,128)S(1)} all-reduce(f32[4,128,3]{2,0,1:T(4,128)S(1)} %copy.41), channel_id=3, replica_groups=mesh['dom'=64,'slab'=8] {'dom'}, use_global_device_ids=true, to_apply=%region_2.3.clone | all-reduce | flops 1536 | bytes 12288
  543.4 14.8 %psum.14 = f32[4,2,3]{2,0,1:T(4,128)S(1)} all-reduce(f32[4,2,3]{2,0,1:T(4,128)S(1)} %constant_dynamic-slice_fusion), channel_id=1, replica_groups=mesh['dom'=64,'slab'=8] {'slab'}, use_global_device_ids=true, to_apply=%region_3.4 | all-reduce | flops 24 | bytes 192 | tf_op jit(solution)/shard_map/psum | solution.py:89
  558.2 0.7 copy.48
  558.9 19.8 %all-reduce.6.cloned.1.call-done = f32[4096,128]{1,0:T(8,128)} async-done(((f32[4096,128]{1,0:T(8,128)}), f32[4096,128]{1,0:T(8,128)}) %all-reduce.6.cloned.1.call-update) | async-done | bytes 2097168 | tf_op jit(solution)/shard_map/psum | solution.py:93
  578.7 1.7 constant_dynamic-slice_fusion.2
  (17 shorter events, 0.1 us)
Async XLA Ops:
  7.2 3.0 copy-start
  7.2 60.0 %copy-start.1 = (bf16[256,3,8,128]{3,2,1,0:T(8,128)(2,1)S(1)}, bf16[256,3,8,128]{3,2,1,0:T(8,128)(2,1)}, u32[]{:S(2)}) copy-start(bf16[256,3,8,128]{3,2,1,0:T(8,128)(2,1)} %param.13) | copy-start | bytes 4718596
  7.2 83.1 %all-reduce.8.cloned.1.call-start = ((), (), s32[]{:S(2)}) async-start(), calls=%async_computation.2 | async-start | bytes 196608
  10.8 59.5 %copy-start.4 = (s32[256]{0:T(256)S(1)}, s32[256]{0:T(256)}, u32[]{:S(2)}) copy-start(s32[256]{0:T(256)} %param.11) | copy-start | bytes 3076
  11.6 277.9 %reduce-scatter.4.cloned.1.call-start = ((), (), s32[]{:S(2)}) async-start(), calls=%async_computation.3 | async-start | bytes 1597440
  150.0 1.7 copy-start.2
  150.0 2.0 copy-start.3
  151.7 427.0 %all-reduce.6.cloned.1.call-start = ((), (), s32[]{:S(2)}) async-start(), calls=%async_computation.1 | async-start | bytes 4194304 | tf_op jit(solution)/shard_map/psum | solution.py:93
Sparse Core Ops, SparseCore 0:
  11.7 78.5 all-reduce.7
  151.8 137.6 reduce-scatter.3
  294.4 284.1 all-reduce.5
where the time goes:
time: 587 us
  blocking collectives  370 us (63%)
  waiting for transfers between devices  177 us (30%)
  local copies, waits for them, and re-layouts  15.6 us (3%)
  between operations  15.2 us (3%)
    unnamed x1, blocking collectives  246 us
    unnamed x5, waiting for transfers between devices  157 us
    all_gather x1, blocking collectives, shards(): proj_piece = lax.all_gather(projected, 'dom', axis=1, tiled=True)  56 us
    all_gather x1, blocking collectives, shards(): warp_piece = lax.all_gather(warp, 'dom', axis=1, tiled=True)  53.1 us
    psum x1, waiting for transfers between devices, shards(): summed = lax.psum(spread, ('dom', 'slab'))  19.8 us
    psum x1, blocking collectives, shards(): warp_grad = lax.psum(own_warp, 'slab')  14.8 us
  transfers between devices with their start and end apart: 3, of which 3 were waited for; matrix products, arithmetic and copies ran while one was open for 2% of the time, Pallas kernels for 0%

commit v1 on v0

v1 whole, which is shorter than its diff:
```python
import jax
import jax.numpy as jnp
from jax import lax
from jax.experimental import pallas as pl
from jax.experimental.pallas import tpu as pltpu
from jax.sharding import PartitionSpec as P

MESH = pl.DeviceIdType.MESH
F32, BF16 = jnp.float32, jnp.bfloat16
NY, NX, NC, NZ = 8, 4, 2, 8
BOX, TILTS, CTRL, COLS = 64, 3, 4, 128
PARTS = 256
BAND = BOX // NZ
ROWS = TILTS * BAND
OWN = 2
NS = NY * NX * NC * OWN
GROUP = NY * OWN
SLAB = BOX * BOX // NZ
CELLS = BOX * BOX
CPY = COLS // NY

(META_Y, META_X, META_C, PZ, PY, PX, PC, SC, SX, SY, VZ, VC, VX, VY, QC, QX, QY, QZ) = range(18)


def split2(v):
    hi = v.astype(BF16)
    return hi, (v - hi.astype(F32)).astype(BF16)


def split3(v):
    hi = v.astype(BF16)
    rest = v - hi.astype(F32)
    mid = rest.astype(BF16)
    return hi, mid, (rest - mid.astype(F32)).astype(BF16)


def dot(a, b):
    return jnp.dot(a, b, preferred_element_type=F32)


def kernel(
    vol,
    idx,
    frac,
    warp,
    series,
    pos,
    images,
    res_out,
    wg_out,
    back_out,
    imgv,
    xf,
    xt,
    tmp,
    meta,
    psrc,
    prcv,
    pall,
    pgf,
    pf,
    bs,
    brc,
    brx,
    ysrc,
    yrcv,
    wsp,
    zsrc,
    zrcv,
    crcv,
    xrcv,
    vall,
    qsrc,
    qrc,
    qrx,
    qry,
    qrz,
    last,
    rf,
    rb,
    ssem,
    rsem,
    lsem,
):
    d, z = lax.axis_index("dom"), lax.axis_index("slab")
    c, x, y = lax.rem(d, NC), lax.rem(d // NC, NX), d // (NC * NX)

    def spot(axis, k):
        at = {"y": y, "x": x, "c": c, "z": z}
        size = {"y": NY, "x": NX, "c": NC, "z": NZ}[axis]
        at[axis] = lax.rem(at[axis] + k, size)
        return ((at["y"] * NX + at["x"]) * NC + at["c"], at["z"]), at[axis]

    def send(row, axis, src, dst):
        size = {"y": NY, "x": NX, "c": NC, "z": NZ}[axis]
        copies = []
        for k in range(1, size):
            device, there = spot(axis, k)
            copy = pltpu.make_async_remote_copy(
                src_ref=src(there),
                dst_ref=dst,
                send_sem=ssem.at[row, k],
                recv_sem=rsem.at[row, k],
                device_id=device,
                device_id_type=MESH,
            )
            copy.start()
            copies.append(copy)
        return copies

    def arrive(copies):
        for copy in copies:
            copy.wait_recv()

    sent = []

    barrier = pltpu.get_barrier_semaphore()
    for axis, size in (("y", NY), ("x", NX), ("c", NC), ("z", NZ)):
        for k in range(1, size):
            pl.semaphore_signal(barrier, inc=1, device_id=spot(axis, k)[0], device_id_type=MESH)

    image_copy = pltpu.make_async_copy(images, imgv, lsem.at[0])
    image_copy.start()

    lane8 = lax.broadcasted_iota(jnp.int32, (8, COLS), 1)
    tmp[...] = jnp.zeros_like(tmp)
    for q in range(OWN):
        tmp[0, q * 4 : q * 4 + 3, 0:BOX] = idx[q].astype(F32)
        tmp[1, q * 4 : q * 4 + 3, 0:BOX] = frac[q]
    for k in range(CTRL):
        one = warp[k].astype(F32)
        for q in range(OWN):
            tmp[2, q * 4 + k : q * 4 + k + 1, 0:TILTS] = one[q : q + 1]
    own_idx, own_frac, own_warp = tmp[0], tmp[1], tmp[2]
    band_idx = pltpu.roll(own_idx, lax.rem(COLS - z * BAND, COLS), 1)
    band_frac = pltpu.roll(own_frac, lax.rem(COLS - z * BAND + BAND, COLS), 1)
    rolled_warp = pltpu.roll(own_warp, 2 * BAND, 1)
    meta[c, x, y] = jnp.where(
        lane8 < BAND, band_idx, jnp.where(lane8 < 2 * BAND, band_frac, rolled_warp)
    )

    columns = jnp.transpose(jnp.where(lane8 < BOX, own_idx, pltpu.roll(own_frac, BOX, 1)))
    cell = (lax.broadcasted_iota(jnp.int32, (BOX, SLAB), 1) + z * SLAB).astype(F32)
    volume = vol[...]
    for q in range(OWN):
        for t in range(TILTS):
            low = columns[0:BOX, q * 4 + t : q * 4 + t + 1]
            part = columns[BOX : 2 * BOX, q * 4 + t : q * 4 + t + 1]
            weight = jnp.where(cell == low, 1.0 - part, 0.0) + jnp.where(cell == low + BOX, part, 0.0)
            hi, mid, lo = split3(weight)
            value = dot(hi, volume) + (dot(mid, volume) + dot(lo, volume))
            psrc[q * TILTS + t] = value.reshape(NZ, BAND, COLS)

    pl.semaphore_wait(barrier, NY + NX + NC + NZ - 4)
    meta_y = send(META_Y, "y", lambda there: meta.at[c, x, y], meta.at[c, x, y])
    p_z = send(PZ, "z", lambda there: psrc.at[:, there], prcv.at[z])
    sent += meta_y + p_z

    image_copy.wait()

    def widen(i, _):
        part = imgv[pl.ds(i * 32, 32)].astype(F32)
        xf[pl.ds(pl.multiple_of(i * 32 * ROWS, 32 * ROWS), 32 * ROWS), :] = part.reshape(32 * ROWS, COLS)
        return 0

    lax.fori_loop(0, PARTS // 32, widen, 0)

    def gather_rows(r, _):
        xt[r] = xf[pl.ds(r, PARTS, stride=ROWS), :].astype(BF16)
        return 0

    lax.fori_loop(0, ROWS, gather_rows, 0)

    arrive(meta_y)
    meta_x = send(META_X, "x", lambda there: meta.at[c, x], meta.at[c, x])
    sent += meta_x

    row = lax.broadcasted_iota(jnp.int32, (NS, PARTS), 0)
    name = (
        lax.rem(row, GROUP) // OWN * (NX * NC * OWN)
        + lax.rem(row // GROUP, NX) * (NC * OWN)
        + row // (GROUP * NX) * OWN
        + lax.rem(row, OWN)
    )
    hit = series[...].reshape(1, PARTS) == name
    hot = hit.astype(F32)
    hot16 = hot.astype(BF16)
    at = pos[...].reshape(1, PARTS)
    remain = 1.0 - at
    square = at * at
    cubed = square * at
    basis = [
        remain * remain * remain / 6.0,
        (3.0 * cubed - 6.0 * square + 4.0) / 6.0,
        (-3.0 * cubed + 3.0 * square + 3.0 * at + 1.0) / 6.0,
        cubed / 6.0,
    ]

    arrive(p_z)
    own = psrc[:, z]
    for k in range(1, NZ):
        own = own + prcv[lax.rem(z + k, NZ)]
    pall[c, x, y] = own.reshape(OWN * ROWS, COLS).astype(BF16)
    p_y = send(PY, "y", lambda there: pall.at[c, x, y], pall.at[c, x, y])
    sent += p_y

    arrive(meta_x)
    meta_c = send(META_C, "c", lambda there: meta.at[c], meta.at[c])
    sent += meta_c
    arrive(meta_c)

    flat_meta = meta.reshape(NS * 4, COLS)
    lane = lax.broadcasted_iota(jnp.int32, (NS, COLS), 1)
    table = jnp.zeros((NS, COLS), F32)
    for k in range(CTRL):
        rows = pltpu.roll(flat_meta[pl.ds(k, NS, stride=4), :], COLS - 2 * BAND + 3 * k, 1)
        table = jnp.where((lane >= 3 * k) & (lane < 3 * k + 3), rows, table)
    chosen = dot(jnp.transpose(table)[0:16].astype(BF16), hot16)
    scale = [
        sum(basis[k] * chosen[3 * k + t : 3 * k + t + 1] for k in range(CTRL)) for t in range(TILTS)
    ]

    squares = jnp.zeros((NS, COLS), F32)
    for t in range(TILTS):
        weight = jnp.where(hit, scale[t], 0.0)
        squares = jnp.where(lane == t, jnp.sum(weight * weight, axis=1, keepdims=True), squares)
        both = jnp.concatenate(split2(weight), axis=0)
        for u in range(0, BAND, 2):
            r = t * BAND + u
            pair = dot(both, jnp.concatenate([xt[r], xt[r + 1]], axis=1))
            pair = pair[:NS] + pair[NS:]
            bs[:, r] = pair[:, :COLS].reshape(NC * NX, GROUP, COLS)
            bs[:, r + 1] = pair[:, COLS:].reshape(NC * NX, GROUP, COLS)
    bs[:, ROWS] = squares.reshape(NC * NX, GROUP, COLS)

    other, there = spot("c", 1)
    c_copies = []
    for k in range(NX):
        to = lax.rem(x + 1 + k, NX)
        copy = pltpu.make_async_remote_copy(
            src_ref=bs.at[there * NX + to],
            dst_ref=brc.at[to],
            send_sem=ssem.at[SC, k],
            recv_sem=rsem.at[SC, k],
            device_id=other,
            device_id_type=MESH,
        )
        copy.start()
        c_copies.append(copy)
    sent += c_copies
    x_copies = []
    for k in range(NX):
        to = lax.rem(x + 1 + k, NX)
        c_copies[k].wait_recv()
        brc[to] = brc[to] + bs[c * NX + to]
        if k < NX - 1:
            copy = pltpu.make_async_remote_copy(
                src_ref=brc.at[to],
                dst_ref=brx.at[x],
                send_sem=ssem.at[SX, k + 1],
                recv_sem=rsem.at[SX, k + 1],
                device_id=spot("x", k + 1)[0],
                device_id_type=MESH,
            )
            copy.start()
            x_copies.append(copy)
    sent += x_copies

    flat_group = meta.at[c, x].reshape(NY * 8, COLS)
    cells = lax.broadcasted_iota(jnp.int32, (GROUP, CELLS), 1).astype(F32)
    for t in range(TILTS):
        group = flat_group[pl.ds(t, GROUP, stride=4), :]
        for u in range(BAND):
            low = group[:, u : u + 1]
            part = group[:, BAND + u : BAND + u + 1]
            weight = jnp.where(
                cells == low, 1.0 - part, jnp.where(cells == low + BOX, part, 0.0)
            )
            wsp[(t * BAND + u) * GROUP : (t * BAND + u + 1) * GROUP, :] = weight.astype(BF16)

    arrive(p_y)
    pgf[...] = pall[c, x].reshape(GROUP * ROWS, COLS).astype(F32)

    arrive(x_copies)
    total = brc[x]
    for k in range(1, NX):
        total = total + brx[lax.rem(x + k, NX)]
    squares = total[ROWS]
    fixed = []
    for t in range(TILTS):
        for u in range(BAND):
            r = t * BAND + u
            fixed.append(total[r] - squares[:, t : t + 1] * pgf[pl.ds(r, GROUP, stride=ROWS), :])
    turned = jnp.transpose(jnp.concatenate(fixed, axis=0))
    ysrc[...] = turned.reshape(NY, CPY, ROWS * GROUP).astype(BF16)
    s_y = send(SY, "y", lambda there: ysrc.at[there], yrcv.at[y])
    p_x = send(PX, "x", lambda there: pall.at[c, x], pall.at[c, x])
    sent += s_y + p_x

    arrive(s_y)
    total = ysrc[y].astype(F32)
    for k in range(1, NY):
        total = total + yrcv[lax.rem(y + k, NY)].astype(F32)
    both = jnp.concatenate(split2(total), axis=0)
    for k in range(NZ):
        part = dot(both, wsp[:, k * SLAB : (k + 1) * SLAB])
        zsrc[k] = (part[:CPY] + part[CPY:]).astype(BF16)
    v_z = send(VZ, "z", lambda there: zsrc.at[there], zrcv.at[z])
    sent += v_z

    arrive(p_x)
    p_c = send(PC, "c", lambda there: pall.at[c], pall.at[c])
    sent += p_c
    arrive(p_c)
    pf[...] = pall[...].reshape(NS * ROWS, COLS).astype(F32)
    hot_turned = jnp.transpose(hot).astype(BF16)
    lane_p = lax.broadcasted_iota(jnp.int32, (PARTS, COLS), 1)
    turned = jnp.transpose(jnp.concatenate(scale + basis + [basis[0]], axis=0))
    inner = jnp.zeros((PARTS, COLS), F32)
    for t in range(TILTS):
        scale_column = turned[:, t : t + 1]

        def one_row(u, acc):
            r = t * BAND + u
            guess = dot(hot_turned, pf[pl.ds(r, NS, stride=ROWS), :].astype(BF16))
            left = (xt[r].astype(F32) - scale_column * guess).astype(BF16).astype(F32)
            rf[pl.ds(r, PARTS, stride=ROWS), :] = left
            return acc + left * guess

        acc = lax.fori_loop(0, BAND, one_row, jnp.zeros((PARTS, COLS), F32))
        inner = jnp.where(lax.rem(lane_p, TILTS) == t, jnp.sum(acc, axis=1, keepdims=True), inner)

    def narrow(i, _):
        part = rf[pl.ds(pl.multiple_of(i * 32 * ROWS, 32 * ROWS), 32 * ROWS), :]
        rb[pl.ds(i * 32, 32)] = part.reshape(32, TILTS, BAND, COLS).astype(BF16)
        return 0

    lax.fori_loop(0, PARTS // 32, narrow, 0)
    res_copy = pltpu.make_async_copy(rb, res_out, lsem.at[1])
    res_copy.start()
    term = jnp.zeros((PARTS, COLS), F32)
    for k in range(CTRL):
        term = jnp.where(lane_p // TILTS == k, turned[:, TILTS + k : TILTS + k + 1] * inner, term)
    hi, mid, lo = split3(term)
    grad = (dot(hot16, hi) + (dot(hot16, mid) + dot(hot16, lo))) * (-1.0 / (BOX * BOX))
    qsrc[...] = grad.reshape(NC, NX, GROUP, COLS)
    q_c = send(QC, "c", lambda there: qsrc.at[there], qrc)
    sent += q_c

    arrive(v_z)
    total = zsrc[z].astype(F32)
    for k in range(1, NZ):
        total = total + zrcv[lax.rem(z + k, NZ)].astype(F32)
    crcv[c] = total
    v_c = send(VC, "c", lambda there: crcv.at[c], crcv.at[c])
    sent += v_c
    arrive(q_c)
    qrc[...] = qrc[...] + qsrc[c]
    q_x = send(QX, "x", lambda there: qrc.at[there], qrx.at[x])
    sent += q_x
    arrive(v_c)
    xrcv[x] = crcv[0] + crcv[1]
    v_x = send(VX, "x", lambda there: xrcv.at[x], xrcv.at[x])
    sent += v_x
    arrive(q_x)
    total = qrc[x]
    for k in range(1, NX):
        total = total + qrx[lax.rem(x + k, NX)]
    qry[y] = total
    q_y = send(QY, "y", lambda there: qry.at[y], qry.at[y])
    sent += q_y
    arrive(v_x)
    vall[y] = ((xrcv[0] + xrcv[1]) + (xrcv[2] + xrcv[3])).astype(BF16)
    v_y = send(VY, "y", lambda there: vall.at[y], vall.at[y])
    sent += v_y
    arrive(q_y)
    total = qry[0]
    for k in range(1, NY):
        total = total + qry[k]
    qrz[z] = total
    q_z = send(QZ, "z", lambda there: qrz.at[z], qrz.at[z])
    sent += q_z
    arrive(v_y)
    back_out[...] = jnp.transpose(vall[...].astype(F32).reshape(COLS, SLAB))
    arrive(q_z)
    total = qrz[0]
    for k in range(1, NZ):
        total = total + qrz[k]
    last[...] = total
    mine = last[pl.ds(y * OWN, OWN), :]
    for k in range(CTRL):
        wg_out[k] = pltpu.roll(mine, (COLS - TILTS * k) % COLS, 1)[:, 0:TILTS]
    res_copy.wait()
    for copy in sent:
        copy.wait_send()


def shards(reference_volume, cell_index, cell_frac, warp, series, position, images):
    vmem = pl.BlockSpec(memory_space=pltpu.VMEM)
    hbm = pl.BlockSpec(memory_space=pl.ANY)
    scratch = [
        pltpu.VMEM((PARTS, TILTS, BAND, COLS), BF16),
        pltpu.VMEM((PARTS * ROWS, COLS), F32),
        pltpu.VMEM((ROWS, PARTS, COLS), BF16),
        pltpu.VMEM((3, 8, COLS), F32),
        pltpu.VMEM((NC, NX, NY, 8, COLS), F32),
        pltpu.VMEM((OWN * TILTS, NZ, BAND, COLS), F32),
        pltpu.VMEM((NZ, OWN * TILTS, BAND, COLS), F32),
        pltpu.VMEM((NC, NX, NY, OWN * ROWS, COLS), BF16),
        pltpu.VMEM((GROUP * ROWS, COLS), F32),
        pltpu.VMEM((NS * ROWS, COLS), F32),
        pltpu.VMEM((NC * NX, ROWS + 1, GROUP, COLS), F32),
        pltpu.VMEM((NX, ROWS + 1, GROUP, COLS), F32),
        pltpu.VMEM((NX, ROWS + 1, GROUP, COLS), F32),
        pltpu.VMEM((NY, CPY, ROWS * GROUP), BF16),
        pltpu.VMEM((NY, CPY, ROWS * GROUP), BF16),
        pltpu.VMEM((ROWS * GROUP, CELLS), BF16),
        pltpu.VMEM((NZ, CPY, SLAB), BF16),
        pltpu.VMEM((NZ, CPY, SLAB), BF16),
        pltpu.VMEM((NC, CPY, SLAB), F32),
        pltpu.VMEM((NX, CPY, SLAB), F32),
        pltpu.VMEM((NY, CPY, SLAB), BF16),
        pltpu.VMEM((NC, NX, GROUP, COLS), F32),
        pltpu.VMEM((NX, GROUP, COLS), F32),
        pltpu.VMEM((NX, GROUP, COLS), F32),
        pltpu.VMEM((NY, GROUP, COLS), F32),
        pltpu.VMEM((NZ, GROUP, COLS), F32),
        pltpu.VMEM((GROUP, COLS), F32),
        pltpu.VMEM((PARTS * ROWS, COLS), F32),
        pltpu.VMEM((PARTS, TILTS, BAND, COLS), BF16),
        pltpu.SemaphoreType.DMA((18, 8)),
        pltpu.SemaphoreType.DMA((18, 8)),
        pltpu.SemaphoreType.DMA((2,)),
    ]
    return pl.pallas_call(
        kernel,
        out_shape=(
            jax.ShapeDtypeStruct((PARTS, TILTS, BAND, COLS), BF16),
            jax.ShapeDtypeStruct((CTRL, OWN, TILTS), F32),
            jax.ShapeDtypeStruct((SLAB, COLS), F32),
        ),
        in_specs=[vmem] * 6 + [hbm],
        out_specs=(hbm, vmem, vmem),
        scratch_shapes=scratch,
        compiler_params=pltpu.CompilerParams(
            collective_id=0, has_side_effects=True, vmem_limit_bytes=56 << 20
        ),
        name="refine",
    )(reference_volume, cell_index, cell_frac, warp, series, position, images)


def solution(mesh):
    placed = (
        P("slab", None),
        P("dom", None, None),
        P("dom", None, None),
        P(None, "dom", None),
        P("dom"),
        P("dom"),
        P("dom", None, "slab", None),
    )
    return jax.shard_map(
        shards,
        mesh=mesh,
        in_specs=placed,
        out_specs=(P("dom", None, "slab", None), P(None, "dom", None), P("slab", None)),
        check_vma=False,
    )
```

time: 587 us -> 78.8 us (0.13)
  the two profiles are of different devices: /device:TPU:1 before, /device:TPU:4 now
where the time goes in v1:
time: 78.8 us; the launch traced here: 78.5 us
  Pallas kernels  69 us (88%)
  local copies, waits for them, and re-layouts  8.82 us (11%)
    pallas_call x1, Pallas kernels, shards(): pl.pallas_call(kernel, out_shape=(jax.ShapeDtypeStruct((PARTS, TILTS, BAN...  69 us
    unnamed x7, local copies, waits for them, and re-layouts  7.48 us

profile of v1, /device:TPU:4, one launch (start us, length us, event | category | flops | bytes accessed | tf_op | source)
XLA Modules:
  0.0 78.5 jit_solution(15923339183585170221)
XLA Ops:
  0.6 1.4 %copy.12.warp = bf16[4,2,3]{2,1,0:T(2,128)(2,1)} copy(bf16[4,2,3]{0,1,2:T(2,128)(2,1)} %param.10) | data formatting | bytes 96 | tf_op args[3]
  2.0 1.3 %copy.10.idx = s32[2,3,64]{2,1,0:T(4,128)} copy(s32[2,3,64]{2,0,1:T(2,128)} %param.8) | data formatting | bytes 3072 | tf_op args[1]
  3.3 1.3 %copy.11.frac = f32[2,3,64]{2,1,0:T(4,128)} copy(f32[2,3,64]{2,0,1:T(2,128)} %param.9) | data formatting | bytes 3072 | tf_op args[2]
  4.5 69.0 %refine.1 = (bf16[256,3,8,128]{3,2,1,0:T(8,128)(2,1)}, f32[4,2,3]{2,1,0:T(2,128)}, f32[512,128]{1,0:T(8,128)}) custom-call(bf16[512,128]{1,0:T(8,128)(2,1)} %vol.1, s32[2,3,64]{2,1,0:T(4,128)} %copy.10.idx, f32[2,3,64]{2,1,0:T(4,128)} %copy.11.frac, bf16[4,2,3]{2,1,0:T(2,128)(2,1)} %copy.12.warp, s32[256]{0:T(256)} %series.1, f32[256]{0:T(256)} %pos.1, ...), custom_call_target="tpu_custom_call" | custom-call | tf_op jit(solution)/shard_map/refine/pallas_call | solution.py:435
  73.6 1.3 %copy.13 = f32[4,2,3]{0,1,2:T(2,128)} copy(f32[4,2,3]{2,1,0:T(2,128)} %get-tuple-element.4) | data formatting | bytes 192 | tf_op jit(solution)/shard_map/refine/pallas_call | solution.py:435
  74.9 0.0 copy-start
  74.9 2.9 %copy.16 = bf16[256,3,8,128]{3,2,1,0:T(8,128)(2,1)} copy(bf16[256,3,8,128]{3,2,1,0:T(8,128)(2,1)} %get-tuple-element.9) | data formatting | bytes 3145728
  77.8 0.0 copy-done
  77.8 0.7 copy.17
Async XLA Ops:
  74.9 2.9 %copy-start = (f32[512,128]{1,0:T(8,128)S(1)}, f32[512,128]{1,0:T(8,128)}, u32[]{:S(2)}) copy-start(f32[512,128]{1,0:T(8,128)} %get-tuple-element.11) | copy-start | bytes 786436

commit v2 on v1

v2 whole, which is shorter than its diff:
```python
import jax
import jax.numpy as jnp
from jax import lax
from jax.experimental import pallas as pl
from jax.experimental.pallas import tpu as pltpu
from jax.sharding import PartitionSpec as P

MESH = pl.DeviceIdType.MESH
F32, BF16 = jnp.float32, jnp.bfloat16
NY, NX, NC, NZ = 8, 4, 2, 8
BOX, TILTS, CTRL, COLS = 64, 3, 4, 128
PARTS = 256
BAND = BOX // NZ
ROWS = TILTS * BAND
OWN = 2
NS = NY * NX * NC * OWN
GROUP = NY * OWN
SLAB = BOX * BOX // NZ
CELLS = BOX * BOX
CPY = COLS // NY

(META_Y, META_X, META_C, PZ, PY, PX, PC, SC, SX, SY, VZ, VC, VX, VY, QC, QX, QY, QZ) = range(18)
LAST = QZ


def split2(v):
    hi = v.astype(BF16)
    return hi, (v - hi.astype(F32)).astype(BF16)


def split3(v):
    hi = v.astype(BF16)
    rest = v - hi.astype(F32)
    mid = rest.astype(BF16)
    return hi, mid, (rest - mid.astype(F32)).astype(BF16)


def dot(a, b):
    return jnp.dot(a, b, preferred_element_type=F32)


def kernel(
    vol_in,
    idx_in,
    frac_in,
    warp_in,
    series_in,
    pos_in,
    images,
    res_out,
    wg_out,
    back_out,
    vol,
    idx,
    frac,
    warp,
    series,
    pos,
    imgv,
    xf,
    xt,
    tmp,
    meta,
    psrc,
    prcv,
    pall,
    pgf,
    pf,
    bs,
    brc,
    brx,
    ysrc,
    yrcv,
    wsp,
    zsrc,
    zrcv,
    crcv,
    xrcv,
    vall,
    qsrc,
    qrc,
    qrx,
    qry,
    qrz,
    last,
    rf,
    rb,
    ssem,
    rsem,
    lsem,
):
    d, z = lax.axis_index("dom"), lax.axis_index("slab")
    c, x, y = lax.rem(d, NC), lax.rem(d // NC, NX), d // (NC * NX)

    def spot(axis, k):
        at = {"y": y, "x": x, "c": c, "z": z}
        size = {"y": NY, "x": NX, "c": NC, "z": NZ}[axis]
        at[axis] = lax.rem(at[axis] + k, size)
        return ((at["y"] * NX + at["x"]) * NC + at["c"], at["z"]), at[axis]

    def remote(row, device, src, dst):
        return pltpu.make_async_remote_copy(
            src_ref=src,
            dst_ref=dst,
            send_sem=ssem.at[row],
            recv_sem=rsem.at[row],
            device_id=device,
            device_id_type=MESH,
        )

    def send(row, axis, src, dst, bulk):
        size = {"y": NY, "x": NX, "c": NC, "z": NZ}[axis]
        for k in range(1, size):
            device, there = spot(axis, k)
            remote(row, device, src(there), dst).start()
        whole = remote(row, spot(axis, 1)[0], bulk, bulk)
        sent.append(whole)
        return whole

    sent = []

    barrier = pltpu.get_barrier_semaphore()
    for axis, size in (("y", NY), ("x", NX), ("c", NC), ("z", NZ)):
        for k in range(1, size):
            pl.semaphore_signal(barrier, inc=1, device_id=spot(axis, k)[0], device_id_type=MESH)

    small_copies = [
        pltpu.make_async_copy(a, b, lsem.at[k])
        for k, (a, b) in enumerate(
            (
                (idx_in, idx),
                (frac_in, frac),
                (warp_in, warp),
                (vol_in, vol),
                (series_in, series),
                (pos_in, pos),
            )
        )
    ]
    for copy in small_copies:
        copy.start()
    step = PARTS // 8
    for k in range(8):
        rows = pl.ds(k * step, step)
        pltpu.make_async_copy(images.at[rows], imgv.at[rows], lsem.at[6]).start()

    lane8 = lax.broadcasted_iota(jnp.int32, (8, COLS), 1)
    tmp[...] = jnp.zeros_like(tmp)
    for copy in small_copies[:3]:
        copy.wait()
    for q in range(OWN):
        for t in range(TILTS):
            at = q * 4 + t
            tmp[0, at : at + 1, 0:BOX] = idx[t, q : q + 1].astype(F32)
            tmp[1, at : at + 1, 0:BOX] = frac[t, q : q + 1]
            tmp[2, at : at + 1, 0:CTRL] = warp[t].astype(F32)[q : q + 1]
    own_idx, own_frac, own_warp = tmp[0], tmp[1], tmp[2]
    band_idx = pltpu.roll(own_idx, lax.rem(COLS - z * BAND, COLS), 1)
    band_frac = pltpu.roll(own_frac, lax.rem(COLS - z * BAND + BAND, COLS), 1)
    rolled_warp = pltpu.roll(own_warp, 2 * BAND, 1)
    meta[c, x, y] = jnp.where(
        lane8 < BAND, band_idx, jnp.where(lane8 < 2 * BAND, band_frac, rolled_warp)
    )

    pl.semaphore_wait(barrier, NY + NX + NC + NZ - 4)
    meta_y = send(META_Y, "y", lambda there: meta.at[c, x, y], meta.at[c, x, y], meta.at[0, 0, 0 : NY - 1])

    columns = jnp.transpose(jnp.where(lane8 < BOX, own_idx, pltpu.roll(own_frac, BOX, 1)))
    cell = (lax.broadcasted_iota(jnp.int32, (BOX, SLAB), 1) + z * SLAB).astype(F32)
    small_copies[3].wait()
    volume = vol[...]
    for q in range(OWN):
        for t in range(TILTS):
            low = columns[0:BOX, q * 4 + t : q * 4 + t + 1]
            part = columns[BOX : 2 * BOX, q * 4 + t : q * 4 + t + 1]
            weight = jnp.where(cell == low, 1.0 - part, 0.0) + jnp.where(cell == low + BOX, part, 0.0)
            hi, mid, lo = split3(weight)
            value = dot(hi, volume) + (dot(mid, volume) + dot(lo, volume))
            psrc[q * TILTS + t] = value.reshape(NZ, BAND, COLS)

    p_z = send(PZ, "z", lambda there: psrc.at[:, there], prcv.at[z], prcv.at[0 : NZ - 1])

    pltpu.make_async_copy(images, imgv, lsem.at[6]).wait()
    for copy in small_copies[4:]:
        copy.wait()

    def widen(i, _):
        part = imgv[pl.ds(i * 32, 32)].astype(F32)
        xf[pl.ds(pl.multiple_of(i * 32 * ROWS, 32 * ROWS), 32 * ROWS), :] = part.reshape(32 * ROWS, COLS)
        return 0

    lax.fori_loop(0, PARTS // 32, widen, 0)

    def gather_rows(r, _):
        xt[r] = xf[pl.ds(r, PARTS, stride=ROWS), :].astype(BF16)
        return 0

    lax.fori_loop(0, ROWS, gather_rows, 0)

    meta_y.wait_recv()
    meta_x = send(META_X, "x", lambda there: meta.at[c, x], meta.at[c, x], meta.at[0, 0 : NX - 1])

    row = lax.broadcasted_iota(jnp.int32, (NS, PARTS), 0)
    name = (
        lax.rem(row, GROUP) // OWN * (NX * NC * OWN)
        + lax.rem(row // GROUP, NX) * (NC * OWN)
        + row // (GROUP * NX) * OWN
        + lax.rem(row, OWN)
    )
    hit = series[...].reshape(1, PARTS) == name
    hot = hit.astype(F32)
    hot16 = hot.astype(BF16)
    at = pos[...].reshape(1, PARTS)
    remain = 1.0 - at
    square = at * at
    cubed = square * at
    basis = [
        remain * remain * remain / 6.0,
        (3.0 * cubed - 6.0 * square + 4.0) / 6.0,
        (-3.0 * cubed + 3.0 * square + 3.0 * at + 1.0) / 6.0,
        cubed / 6.0,
    ]

    p_z.wait_recv()
    own = psrc[:, z]
    for k in range(1, NZ):
        own = own + prcv[lax.rem(z + k, NZ)]
    pall[c, x, y] = own.reshape(OWN * ROWS, COLS).astype(BF16)
    p_y = send(PY, "y", lambda there: pall.at[c, x, y], pall.at[c, x, y], pall.at[0, 0, 0 : NY - 1])

    meta_x.wait_recv()
    meta_c = send(META_C, "c", lambda there: meta.at[c], meta.at[c], meta.at[0])
    meta_c.wait_recv()

    flat_meta = meta.reshape(NS * 4, COLS)
    lane = lax.broadcasted_iota(jnp.int32, (NS, COLS), 1)
    table = jnp.zeros((NS, COLS), F32)
    for t in range(TILTS):
        rows = pltpu.roll(flat_meta[pl.ds(t, NS, stride=4), :], COLS - 2 * BAND + CTRL * t, 1)
        table = jnp.where(lane // CTRL == t, rows, table)
    chosen = dot(jnp.transpose(table)[0:16].astype(BF16), hot16)
    scale = [
        sum(basis[k] * chosen[CTRL * t + k : CTRL * t + k + 1] for k in range(CTRL))
        for t in range(TILTS)
    ]

    squares = jnp.zeros((NS, COLS), F32)
    for t in range(TILTS):
        weight = jnp.where(hit, scale[t], 0.0)
        squares = jnp.where(lane == t, jnp.sum(weight * weight, axis=1, keepdims=True), squares)
        both = jnp.concatenate(split2(weight), axis=0)
        for u in range(0, BAND, 2):
            r = t * BAND + u
            pair = dot(both, jnp.concatenate([xt[r], xt[r + 1]], axis=1))
            pair = pair[:NS] + pair[NS:]
            bs[:, r] = pair[:, :COLS].reshape(NC * NX, GROUP, COLS)
            bs[:, r + 1] = pair[:, COLS:].reshape(NC * NX, GROUP, COLS)
    bs[:, ROWS] = squares.reshape(NC * NX, GROUP, COLS)

    p_y.wait_recv()
    p_x = send(PX, "x", lambda there: pall.at[c, x], pall.at[c, x], pall.at[0, 0 : NX - 1])

    other, there = spot("c", 1)
    c_copies = []
    for k in range(NX):
        to = lax.rem(x + 1 + k, NX)
        row = SC if k == 0 else LAST + k
        c_copies.append(remote(row, other, bs.at[there * NX + to], brc.at[to]))
        c_copies[k].start()
    for k in range(NX):
        to = lax.rem(x + 1 + k, NX)
        c_copies[k].wait_recv()
        brc[to] = brc[to] + bs[c * NX + to]
        if k < NX - 1:
            remote(SX, spot("x", k + 1)[0], brc.at[to], brx.at[x]).start()
    s_x = remote(SX, other, brx.at[0 : NX - 1], brx.at[0 : NX - 1])
    sent += c_copies + [s_x]

    pgf[...] = pall[c, x].reshape(GROUP * ROWS, COLS).astype(F32)

    flat_group = meta.at[c, x].reshape(NY * 8, COLS)
    cells = lax.broadcasted_iota(jnp.int32, (GROUP, CELLS), 1).astype(F32)
    for t in range(TILTS):
        group = flat_group[pl.ds(t, GROUP, stride=4), :]
        for u in range(BAND):
            low = group[:, u : u + 1]
            part = group[:, BAND + u : BAND + u + 1]
            weight = jnp.where(
                cells == low, 1.0 - part, jnp.where(cells == low + BOX, part, 0.0)
            )
            wsp[(t * BAND + u) * GROUP : (t * BAND + u + 1) * GROUP, :] = weight.astype(BF16)

    p_x.wait_recv()
    p_c = send(PC, "c", lambda there: pall.at[c], pall.at[c], pall.at[0])
    hot_turned = jnp.transpose(hot).astype(BF16)
    lane_p = lax.broadcasted_iota(jnp.int32, (PARTS, COLS), 1)
    turned = jnp.transpose(jnp.concatenate(scale + basis + [basis[0]], axis=0))
    inner = jnp.zeros((PARTS, COLS), F32)
    p_c.wait_recv()
    pf[...] = pall[...].reshape(NS * ROWS, COLS).astype(F32)
    for t in range(TILTS):
        scale_column = turned[:, t : t + 1]
        acc = jnp.zeros((PARTS, COLS), F32)
        for u in range(0, BAND, 2):
            r = t * BAND + u
            pair = [pf[pl.ds(r + k, NS, stride=ROWS), :].astype(BF16) for k in range(2)]
            guesses = dot(hot_turned, jnp.concatenate(pair, axis=1))
            for k in range(2):
                guess = guesses[:, k * COLS : (k + 1) * COLS]
                left = (xt[r + k].astype(F32) - scale_column * guess).astype(BF16).astype(F32)
                rf[(r + k) * PARTS : (r + k + 1) * PARTS, :] = left
                acc = acc + left * guess
        inner = jnp.where(lane_p // CTRL == t, jnp.sum(acc, axis=1, keepdims=True), inner)

    def narrow(i, _):
        for k in range(16):
            part = rf[pl.ds(i * 16 + k, ROWS, stride=PARTS), :]
            rb[i * 16 + k] = part.reshape(TILTS, BAND, COLS).astype(BF16)
        return 0

    lax.fori_loop(0, PARTS // 16, narrow, 0)
    for k in range(8):
        rows = pl.ds(k * step, step)
        pltpu.make_async_copy(rb.at[rows], res_out.at[rows], lsem.at[7]).start()
    term = jnp.zeros((PARTS, COLS), F32)
    for k in range(CTRL):
        term = jnp.where(lax.rem(lane_p, CTRL) == k, turned[:, TILTS + k : TILTS + k + 1] * inner, term)
    hi, mid, lo = split3(term)
    grad = (dot(hot16, hi) + (dot(hot16, mid) + dot(hot16, lo))) * (-1.0 / (BOX * BOX))
    qsrc[...] = grad.reshape(NC, NX, GROUP, COLS)
    q_c = send(QC, "c", lambda there: qsrc.at[there], qrc, qrc)

    s_x.wait_recv()
    total = brc[x]
    for k in range(1, NX):
        total = total + brx[lax.rem(x + k, NX)]
    squares = total[ROWS]
    fixed = []
    for t in range(TILTS):
        for u in range(BAND):
            r = t * BAND + u
            fixed.append(total[r] - squares[:, t : t + 1] * pgf[pl.ds(r, GROUP, stride=ROWS), :])
    turned = jnp.transpose(jnp.concatenate(fixed, axis=0))
    ysrc[...] = turned.reshape(NY, CPY, ROWS * GROUP).astype(BF16)
    s_y = send(SY, "y", lambda there: ysrc.at[there], yrcv.at[y], yrcv.at[0 : NY - 1])

    q_c.wait_recv()
    qrc[...] = qrc[...] + qsrc[c]
    q_x = send(QX, "x", lambda there: qrc.at[there], qrx.at[x], qrx.at[0 : NX - 1])
    s_y.wait_recv()
    total = ysrc[y].astype(F32)
    for k in range(1, NY):
        total = total + yrcv[lax.rem(y + k, NY)].astype(F32)
    both = jnp.concatenate(split2(total), axis=0)
    for k in range(NZ):
        part = dot(both, wsp[:, k * SLAB : (k + 1) * SLAB])
        zsrc[k] = (part[:CPY] + part[CPY:]).astype(BF16)
    v_z = send(VZ, "z", lambda there: zsrc.at[there], zrcv.at[z], zrcv.at[0 : NZ - 1])

    q_x.wait_recv()
    total = qrc[x]
    for k in range(1, NX):
        total = total + qrx[lax.rem(x + k, NX)]
    qry[y] = total
    q_y = send(QY, "y", lambda there: qry.at[y], qry.at[y], qry.at[0 : NY - 1])
    v_z.wait_recv()
    total = zsrc[z].astype(F32)
    for k in range(1, NZ):
        total = total + zrcv[lax.rem(z + k, NZ)].astype(F32)
    crcv[c] = total
    v_c = send(VC, "c", lambda there: crcv.at[c], crcv.at[c], crcv.at[0])
    q_y.wait_recv()
    total = qry[0]
    for k in range(1, NY):
        total = total + qry[k]
    qrz[z] = total
    q_z = send(QZ, "z", lambda there: qrz.at[z], qrz.at[z], qrz.at[0 : NZ - 1])
    v_c.wait_recv()
    xrcv[x] = crcv[0] + crcv[1]
    v_x = send(VX, "x", lambda there: xrcv.at[x], xrcv.at[x], xrcv.at[0 : NX - 1])
    v_x.wait_recv()
    vall[y] = ((xrcv[0] + xrcv[1]) + (xrcv[2] + xrcv[3])).astype(BF16)
    v_y = send(VY, "y", lambda there: vall.at[y], vall.at[y], vall.at[0 : NY - 1])
    q_z.wait_recv()
    total = qrz[0]
    for k in range(1, NZ):
        total = total + qrz[k]
    last[...] = total
    mine = last[pl.ds(y * OWN, OWN), :]
    for t in range(TILTS):
        wg_out[t] = pltpu.roll(mine, (COLS - CTRL * t) % COLS, 1)[:, 0:CTRL]
    v_y.wait_recv()
    back_out[...] = jnp.transpose(vall[...].astype(F32).reshape(COLS, SLAB))
    pltpu.make_async_copy(rb, res_out, lsem.at[7]).wait()
    for copy in sent:
        copy.wait_send()


def hand_over(res_in, grad_in, back_in, res_out, grad_out, back_out, res, grad, back, isem, osem):
    part = PARTS // 8
    ways = [(grad_in, grad, grad_out), (back_in, back, back_out)]
    for k in range(8):
        rows = pl.ds(k * part, part)
        ways.append((res_in.at[rows], res.at[rows], res_out.at[rows]))
    inward = [pltpu.make_async_copy(a, b, isem.at[k]) for k, (a, b, _) in enumerate(ways)]
    outward = [pltpu.make_async_copy(b, c, osem.at[k]) for k, (_, b, c) in enumerate(ways)]
    for copy in inward:
        copy.start()
    for first, second in zip(inward, outward):
        first.wait()
        second.start()
    for copy in outward:
        copy.wait()


def shards(reference_volume, cell_index, cell_frac, warp, series, position, images):
    vmem = pl.BlockSpec(memory_space=pltpu.VMEM)
    hbm = pl.BlockSpec(memory_space=pl.ANY)
    scratch = [
        pltpu.VMEM((SLAB, COLS), BF16),
        pltpu.VMEM((TILTS, OWN, BOX), jnp.int32),
        pltpu.VMEM((TILTS, OWN, BOX), F32),
        pltpu.VMEM((TILTS, OWN, CTRL), BF16),
        pltpu.VMEM((PARTS,), jnp.int32),
        pltpu.VMEM((PARTS,), F32),
        pltpu.VMEM((PARTS, TILTS, BAND, COLS), BF16),
        pltpu.VMEM((PARTS * ROWS, COLS), F32),
        pltpu.VMEM((ROWS, PARTS, COLS), BF16),
        pltpu.VMEM((3, 8, COLS), F32),
        pltpu.VMEM((NC, NX, NY, 8, COLS), F32),
        pltpu.VMEM((OWN * TILTS, NZ, BAND, COLS), F32),
        pltpu.VMEM((NZ, OWN * TILTS, BAND, COLS), F32),
        pltpu.VMEM((NC, NX, NY, OWN * ROWS, COLS), BF16),
        pltpu.VMEM((GROUP * ROWS, COLS), F32),
        pltpu.VMEM((NS * ROWS, COLS), F32),
        pltpu.VMEM((NC * NX, ROWS + 1, GROUP, COLS), F32),
        pltpu.VMEM((NX, ROWS + 1, GROUP, COLS), F32),
        pltpu.VMEM((NX, ROWS + 1, GROUP, COLS), F32),
        pltpu.VMEM((NY, CPY, ROWS * GROUP), BF16),
        pltpu.VMEM((NY, CPY, ROWS * GROUP), BF16),
        pltpu.VMEM((ROWS * GROUP, CELLS), BF16),
        pltpu.VMEM((NZ, CPY, SLAB), BF16),
        pltpu.VMEM((NZ, CPY, SLAB), BF16),
        pltpu.VMEM((NC, CPY, SLAB), F32),
        pltpu.VMEM((NX, CPY, SLAB), F32),
        pltpu.VMEM((NY, CPY, SLAB), BF16),
        pltpu.VMEM((NC, NX, GROUP, COLS), F32),
        pltpu.VMEM((NX, GROUP, COLS), F32),
        pltpu.VMEM((NX, GROUP, COLS), F32),
        pltpu.VMEM((NY, GROUP, COLS), F32),
        pltpu.VMEM((NZ, GROUP, COLS), F32),
        pltpu.VMEM((GROUP, COLS), F32),
        pltpu.VMEM((PARTS * ROWS, COLS), F32),
        pltpu.VMEM((PARTS, TILTS, BAND, COLS), BF16),
        pltpu.SemaphoreType.DMA((LAST + NX,)),
        pltpu.SemaphoreType.DMA((LAST + NX,)),
        pltpu.SemaphoreType.DMA((8,)),
    ]
    residual, warp_grad, back_volume = pl.pallas_call(
        kernel,
        out_shape=(
            jax.ShapeDtypeStruct((PARTS, TILTS, BAND, COLS), BF16),
            jax.ShapeDtypeStruct((TILTS, OWN, CTRL), F32),
            jax.ShapeDtypeStruct((SLAB, COLS), F32),
        ),
        in_specs=[hbm] * 7,
        out_specs=(hbm, vmem, vmem),
        scratch_shapes=scratch,
        compiler_params=pltpu.CompilerParams(
            collective_id=0, has_side_effects=True, vmem_limit_bytes=56 << 20
        ),
        name="refine",
    )(
        reference_volume,
        jnp.transpose(cell_index, (1, 0, 2)),
        jnp.transpose(cell_frac, (1, 0, 2)),
        jnp.transpose(warp, (2, 1, 0)),
        series,
        position,
        images,
    )
    residual, warp_grad, back_volume = pl.pallas_call(
        hand_over,
        out_shape=(
            jax.ShapeDtypeStruct(residual.shape, BF16),
            jax.ShapeDtypeStruct(warp_grad.shape, F32),
            jax.ShapeDtypeStruct(back_volume.shape, F32),
        ),
        in_specs=[hbm] * 3,
        out_specs=(hbm, hbm, hbm),
        scratch_shapes=[
            pltpu.VMEM(residual.shape, BF16),
            pltpu.VMEM(warp_grad.shape, F32),
            pltpu.VMEM(back_volume.shape, F32),
            pltpu.SemaphoreType.DMA((10,)),
            pltpu.SemaphoreType.DMA((10,)),
        ],
        name="hand_over",
    )(residual, warp_grad, back_volume)
    return residual, jnp.transpose(warp_grad, (2, 1, 0)), back_volume


def solution(mesh):
    placed = (
        P("slab", None),
        P("dom", None, None),
        P("dom", None, None),
        P(None, "dom", None),
        P("dom"),
        P("dom"),
        P("dom", None, "slab", None),
    )
    return jax.shard_map(
        shards,
        mesh=mesh,
        in_specs=placed,
        out_specs=(P("dom", None, "slab", None), P(None, "dom", None), P("slab", None)),
        check_vma=False,
    )
```

time: 78.8 us -> 70.4 us (0.89)
  the two profiles are of different devices: /device:TPU:4 before, /device:TPU:1 now
where the time goes in v2:
time: 70.4 us; the launch traced here: 70.2 us
  Pallas kernels  69.5 us (99%)
    pallas_call x1, Pallas kernels, shards(): pl.pallas_call(kernel, out_shape=(jax.ShapeDtypeStruct((PARTS, TILTS, BAN...  67.2 us
    pallas_call x1, Pallas kernels, shards(): pl.pallas_call(hand_over, out_shape=(jax.ShapeDtypeStruct(residual.shape,...  2.37 us

profile of v2, /device:TPU:1, one launch (start us, length us, event | category | flops | bytes accessed | tf_op | source)
XLA Modules:
  0.0 70.2 jit_solution(16776466309045234527)
XLA Ops:
  0.6 67.2 %refine.1 = (bf16[256,3,8,128]{3,2,1,0:T(8,128)(2,1)}, f32[3,2,4]{2,1,0:T(2,128)}, f32[512,128]{1,0:T(8,128)}) custom-call(bf16[512,128]{1,0:T(8,128)(2,1)} %vol_in.1, s32[3,2,64]{2,1,0:T(2,128)} %bitcast.4, f32[3,2,64]{2,1,0:T(2,128)} %bitcast.5, bf16[3,2,4]{2,1,0:T(2,128)(2,1)} %bitcast.6, s32[256]{0:T(256)} %series_in.1, f32[256]{0:T(256)} %pos_in.1, ...), custom_call_target="tpu_custom_call" | custom-call | tf_op jit(solution)/shard_map/refine/pallas_call | solution.py:459
  67.8 2.4 %hand_over.1 = (bf16[256,3,8,128]{3,2,1,0:T(8,128)(2,1)}, f32[3,2,4]{2,1,0:T(2,128)}, f32[512,128]{1,0:T(8,128)}) custom-call(bf16[256,3,8,128]{3,2,1,0:T(8,128)(2,1)} %get-tuple-element.9.res_in, f32[3,2,4]{2,1,0:T(2,128)} %get-tuple-element.10.grad_in, f32[512,128]{1,0:T(8,128)} %get-tuple-element.11.back_in), custom_call_target="tpu_custom_call" | custom-call | tf_op jit(solution)/shard_map/hand_over/pallas_call | solution.py:482

commit v3 on v2

--- a/solution.py
+++ b/solution.py
@@ -19,8 +19,8 @@
 CELLS = BOX * BOX
 CPY = COLS // NY
 
-(META_Y, META_X, META_C, PZ, PY, PX, PC, SC, SX, SY, VZ, VC, VX, VY, QC, QX, QY, QZ) = range(18)
-LAST = QZ
+(META_Y, META_X, META_C, PZ, PY, PX, PC, VZ, VC, VX, VY, QC, QX, QY, QZ) = range(15)
+SC, SX, SY, EXCHANGES = 15, 15 + TILTS, 15 + 2 * TILTS, 15 + 3 * TILTS
 
 
 def split2(v):
@@ -120,9 +120,13 @@
     sent = []
 
     barrier = pltpu.get_barrier_semaphore()
-    for axis, size in (("y", NY), ("x", NX), ("c", NC), ("z", NZ)):
-        for k in range(1, size):
-            pl.semaphore_signal(barrier, inc=1, device_id=spot(axis, k)[0], device_id_type=MESH)
+    partners = [spot(axis, k)[0] for axis, size in (("c", NC), ("z", NZ)) for k in range(1, size)]
+    plane = []
+    for j in range(1, NY * NX):
+        there = lax.rem(y + j // NX, NY) * NX + lax.rem(x + j % NX, NX)
+        plane.append((there * NC + c, z))
+    for device in partners + plane:
+        pl.semaphore_signal(barrier, inc=1, device_id=device, device_id_type=MESH)
 
     small_copies = [
         pltpu.make_async_copy(a, b, lsem.at[k])
@@ -158,12 +162,16 @@
     band_idx = pltpu.roll(own_idx, lax.rem(COLS - z * BAND, COLS), 1)
     band_frac = pltpu.roll(own_frac, lax.rem(COLS - z * BAND + BAND, COLS), 1)
     rolled_warp = pltpu.roll(own_warp, 2 * BAND, 1)
-    meta[c, x, y] = jnp.where(
+    own_at = x * NY + y
+    meta[c, own_at] = jnp.where(
         lane8 < BAND, band_idx, jnp.where(lane8 < 2 * BAND, band_frac, rolled_warp)
     )
 
-    pl.semaphore_wait(barrier, NY + NX + NC + NZ - 4)
-    meta_y = send(META_Y, "y", lambda there: meta.at[c, x, y], meta.at[c, x, y], meta.at[0, 0, 0 : NY - 1])
+    pl.semaphore_wait(barrier, len(partners + plane))
+    for device in plane:
+        remote(META_Y, device, meta.at[c, own_at], meta.at[c, own_at]).start()
+    meta_p = remote(META_Y, plane[0], meta.at[0, 1:], meta.at[0, 1:])
+    sent.append(meta_p)
 
     columns = jnp.transpose(jnp.where(lane8 < BOX, own_idx, pltpu.roll(own_frac, BOX, 1)))
     cell = (lax.broadcasted_iota(jnp.int32, (BOX, SLAB), 1) + z * SLAB).astype(F32)
@@ -196,9 +204,6 @@
         return 0
 
     lax.fori_loop(0, ROWS, gather_rows, 0)
-
-    meta_y.wait_recv()
-    meta_x = send(META_X, "x", lambda there: meta.at[c, x], meta.at[c, x], meta.at[0, 0 : NX - 1])
 
     row = lax.broadcasted_iota(jnp.int32, (NS, PARTS), 0)
     name = (
@@ -221,14 +226,7 @@
         cubed / 6.0,
     ]
 
-    p_z.wait_recv()
-    own = psrc[:, z]
-    for k in range(1, NZ):
-        own = own + prcv[lax.rem(z + k, NZ)]
-    pall[c, x, y] = own.reshape(OWN * ROWS, COLS).astype(BF16)
-    p_y = send(PY, "y", lambda there: pall.at[c, x, y], pall.at[c, x, y], pall.at[0, 0, 0 : NY - 1])
-
-    meta_x.wait_recv()
+    meta_p.wait_recv()
     meta_c = send(META_C, "c", lambda there: meta.at[c], meta.at[c], meta.at[0])
     meta_c.wait_recv()
 
@@ -244,41 +242,44 @@
         for t in range(TILTS)
     ]
 
-    squares = jnp.zeros((NS, COLS), F32)
+    other, there = spot("c", 1)
+    c_copies, s_x, s_y = [], [], []
     for t in range(TILTS):
         weight = jnp.where(hit, scale[t], 0.0)
-        squares = jnp.where(lane == t, jnp.sum(weight * weight, axis=1, keepdims=True), squares)
+        squares = jnp.sum(weight * weight, axis=1, keepdims=True)
         both = jnp.concatenate(split2(weight), axis=0)
         for u in range(0, BAND, 2):
             r = t * BAND + u
             pair = dot(both, jnp.concatenate([xt[r], xt[r + 1]], axis=1))
             pair = pair[:NS] + pair[NS:]
-            bs[:, r] = pair[:, :COLS].reshape(NC * NX, GROUP, COLS)
-            bs[:, r + 1] = pair[:, COLS:].reshape(NC * NX, GROUP, COLS)
-    bs[:, ROWS] = squares.reshape(NC * NX, GROUP, COLS)
+            bs[:, t, u] = pair[:, :COLS].reshape(NC * NX, GROUP, COLS)
+            bs[:, t, u + 1] = pair[:, COLS:].reshape(NC * NX, GROUP, COLS)
+        bs[:, t, BAND] = jnp.broadcast_to(squares, (NS, COLS)).reshape(NC * NX, GROUP, COLS)
+        c_copies.append(remote(SC + t, other, bs.at[pl.ds(there * NX, NX), t], brc.at[:, t]))
+        c_copies[t].start()
+
+    p_z.wait_recv()
+    own = psrc[:, z]
+    for k in range(1, NZ):
+        own = own + prcv[lax.rem(z + k, NZ)]
+    pall[c, x, y] = own.reshape(OWN * ROWS, COLS).astype(BF16)
+    p_y = send(PY, "y", lambda there: pall.at[c, x, y], pall.at[c, x, y], pall.at[0, 0, 0 : NY - 1])
+
+
+    for t in range(TILTS):
+        c_copies[t].wait_recv()
+        brc[:, t] = brc[:, t] + bs[pl.ds(c * NX, NX), t]
+        bulk = brx.at[0 : NX - 1, t]
+        s_x.append(
+            send(SX + t, "x", lambda there: brc.at[there, t], brx.at[x, t], bulk)
+        )
+    sent += c_copies
 
     p_y.wait_recv()
     p_x = send(PX, "x", lambda there: pall.at[c, x], pall.at[c, x], pall.at[0, 0 : NX - 1])
-
-    other, there = spot("c", 1)
-    c_copies = []
-    for k in range(NX):
-        to = lax.rem(x + 1 + k, NX)
-        row = SC if k == 0 else LAST + k
-        c_copies.append(remote(row, other, bs.at[there * NX + to], brc.at[to]))
-        c_copies[k].start()
-    for k in range(NX):
-        to = lax.rem(x + 1 + k, NX)
-        c_copies[k].wait_recv()
-        brc[to] = brc[to] + bs[c * NX + to]
-        if k < NX - 1:
-            remote(SX, spot("x", k + 1)[0], brc.at[to], brx.at[x]).start()
-    s_x = remote(SX, other, brx.at[0 : NX - 1], brx.at[0 : NX - 1])
-    sent += c_copies + [s_x]
-
     pgf[...] = pall[c, x].reshape(GROUP * ROWS, COLS).astype(F32)
 
-    flat_group = meta.at[c, x].reshape(NY * 8, COLS)
+    flat_group = meta.at[c, pl.ds(x * NY, NY)].reshape(NY * 8, COLS)
     cells = lax.broadcasted_iota(jnp.int32, (GROUP, CELLS), 1).astype(F32)
     for t in range(TILTS):
         group = flat_group[pl.ds(t, GROUP, stride=4), :]
@@ -290,16 +291,47 @@
             )
             wsp[(t * BAND + u) * GROUP : (t * BAND + u + 1) * GROUP, :] = weight.astype(BF16)
 
+    for t in range(TILTS):
+        s_x[t].wait_recv()
+        total = brc[x, t]
+        for k in range(1, NX):
+            total = total + brx[lax.rem(x + k, NX), t]
+        fixed = []
+        for u in range(BAND):
+            guess = pgf[pl.ds(t * BAND + u, GROUP, stride=ROWS), :]
+            fixed.append(total[u] - total[BAND] * guess)
+        turned = jnp.transpose(jnp.concatenate(fixed, axis=0))
+        ysrc[t] = turned.reshape(NY, CPY, BAND * GROUP).astype(BF16)
+        bulk = yrcv.at[t, 0 : NY - 1]
+        s_y.append(
+            send(SY + t, "y", lambda there: ysrc.at[t, there], yrcv.at[t, y], bulk)
+        )
+
+    hot_turned = jnp.transpose(hot).astype(BF16)
+    lane_p = lax.broadcasted_iota(jnp.int32, (PARTS, COLS), 1)
+    factors = jnp.transpose(jnp.concatenate(scale + basis + [basis[0]], axis=0))
+    inner = jnp.zeros((PARTS, COLS), F32)
+
     p_x.wait_recv()
     p_c = send(PC, "c", lambda there: pall.at[c], pall.at[c], pall.at[0])
-    hot_turned = jnp.transpose(hot).astype(BF16)
-    lane_p = lax.broadcasted_iota(jnp.int32, (PARTS, COLS), 1)
-    turned = jnp.transpose(jnp.concatenate(scale + basis + [basis[0]], axis=0))
-    inner = jnp.zeros((PARTS, COLS), F32)
+    totals = []
+    for t in range(TILTS):
+        s_y[t].wait_recv()
+        total = ysrc[t, y].astype(F32)
+        for k in range(1, NY):
+            total = total + yrcv[t, lax.rem(y + k, NY)].astype(F32)
+        totals.append(total)
+    total = jnp.concatenate(totals, axis=1)
+    both = jnp.concatenate(split2(total), axis=0)
+    for k in range(NZ):
+        part = dot(both, wsp[:, k * SLAB : (k + 1) * SLAB])
+        zsrc[k] = (part[:CPY] + part[CPY:]).astype(BF16)
+    v_z = send(VZ, "z", lambda there: zsrc.at[there], zrcv.at[z], zrcv.at[0 : NZ - 1])
+
     p_c.wait_recv()
     pf[...] = pall[...].reshape(NS * ROWS, COLS).astype(F32)
     for t in range(TILTS):
-        scale_column = turned[:, t : t + 1]
+        scale_column = factors[:, t : t + 1]
         acc = jnp.zeros((PARTS, COLS), F32)
         for u in range(0, BAND, 2):
             r = t * BAND + u
@@ -324,63 +356,39 @@
         pltpu.make_async_copy(rb.at[rows], res_out.at[rows], lsem.at[7]).start()
     term = jnp.zeros((PARTS, COLS), F32)
     for k in range(CTRL):
-        term = jnp.where(lax.rem(lane_p, CTRL) == k, turned[:, TILTS + k : TILTS + k + 1] * inner, term)
+        term = jnp.where(lax.rem(lane_p, CTRL) == k, factors[:, TILTS + k : TILTS + k + 1] * inner, term)
     hi, mid, lo = split3(term)
     grad = (dot(hot16, hi) + (dot(hot16, mid) + dot(hot16, lo))) * (-1.0 / (BOX * BOX))
     qsrc[...] = grad.reshape(NC, NX, GROUP, COLS)
     q_c = send(QC, "c", lambda there: qsrc.at[there], qrc, qrc)
 
-    s_x.wait_recv()
-    total = brc[x]
-    for k in range(1, NX):
-        total = total + brx[lax.rem(x + k, NX)]
-    squares = total[ROWS]
-    fixed = []
-    for t in range(TILTS):
-        for u in range(BAND):
-            r = t * BAND + u
-            fixed.append(total[r] - squares[:, t : t + 1] * pgf[pl.ds(r, GROUP, stride=ROWS), :])
-    turned = jnp.transpose(jnp.concatenate(fixed, axis=0))
-    ysrc[...] = turned.reshape(NY, CPY, ROWS * GROUP).astype(BF16)
-    s_y = send(SY, "y", lambda there: ysrc.at[there], yrcv.at[y], yrcv.at[0 : NY - 1])
-
     q_c.wait_recv()
     qrc[...] = qrc[...] + qsrc[c]
     q_x = send(QX, "x", lambda there: qrc.at[there], qrx.at[x], qrx.at[0 : NX - 1])
-    s_y.wait_recv()
-    total = ysrc[y].astype(F32)
-    for k in range(1, NY):
-        total = total + yrcv[lax.rem(y + k, NY)].astype(F32)
-    both = jnp.concatenate(split2(total), axis=0)
-    for k in range(NZ):
-        part = dot(both, wsp[:, k * SLAB : (k + 1) * SLAB])
-        zsrc[k] = (part[:CPY] + part[CPY:]).astype(BF16)
-    v_z = send(VZ, "z", lambda there: zsrc.at[there], zrcv.at[z], zrcv.at[0 : NZ - 1])
-
+    v_z.wait_recv()
+    total = zsrc[z].astype(F32)
+    for k in range(1, NZ):
+        total = total + zrcv[lax.rem(z + k, NZ)].astype(F32)
+    crcv[c] = total
+    v_c = send(VC, "c", lambda there: crcv.at[c], crcv.at[c], crcv.at[0])
+    v_c.wait_recv()
+    xrcv[x] = crcv[0] + crcv[1]
+    v_x = send(VX, "x", lambda there: xrcv.at[x], xrcv.at[x], xrcv.at[0 : NX - 1])
     q_x.wait_recv()
     total = qrc[x]
     for k in range(1, NX):
         total = total + qrx[lax.rem(x + k, NX)]
     qry[y] = total
     q_y = send(QY, "y", lambda there: qry.at[y], qry.at[y], qry.at[0 : NY - 1])
-    v_z.wait_recv()
-    total = zsrc[z].astype(F32)
-    for k in range(1, NZ):
-        total = total + zrcv[lax.rem(z + k, NZ)].astype(F32)
-    crcv[c] = total
-    v_c = send(VC, "c", lambda there: crcv.at[c], crcv.at[c], crcv.at[0])
+    v_x.wait_recv()
+    vall[y] = ((xrcv[0] + xrcv[1]) + (xrcv[2] + xrcv[3])).astype(BF16)
+    v_y = send(VY, "y", lambda there: vall.at[y], vall.at[y], vall.at[0 : NY - 1])
     q_y.wait_recv()
     total = qry[0]
     for k in range(1, NY):
         total = total + qry[k]
     qrz[z] = total
     q_z = send(QZ, "z", lambda there: qrz.at[z], qrz.at[z], qrz.at[0 : NZ - 1])
-    v_c.wait_recv()
-    xrcv[x] = crcv[0] + crcv[1]
-    v_x = send(VX, "x", lambda there: xrcv.at[x], xrcv.at[x], xrcv.at[0 : NX - 1])
-    v_x.wait_recv()
-    vall[y] = ((xrcv[0] + xrcv[1]) + (xrcv[2] + xrcv[3])).astype(BF16)
-    v_y = send(VY, "y", lambda there: vall.at[y], vall.at[y], vall.at[0 : NY - 1])
     q_z.wait_recv()
     total = qrz[0]
     for k in range(1, NZ):
@@ -427,17 +435,17 @@
         pltpu.VMEM((PARTS * ROWS, COLS), F32),
         pltpu.VMEM((ROWS, PARTS, COLS), BF16),
         pltpu.VMEM((3, 8, COLS), F32),
-        pltpu.VMEM((NC, NX, NY, 8, COLS), F32),
+        pltpu.VMEM((NC, NX * NY, 8, COLS), F32),
         pltpu.VMEM((OWN * TILTS, NZ, BAND, COLS), F32),
         pltpu.VMEM((NZ, OWN * TILTS, BAND, COLS), F32),
         pltpu.VMEM((NC, NX, NY, OWN * ROWS, COLS), BF16),
         pltpu.VMEM((GROUP * ROWS, COLS), F32),
         pltpu.VMEM((NS * ROWS, COLS), F32),
-        pltpu.VMEM((NC * NX, ROWS + 1, GROUP, COLS), F32),
-        pltpu.VMEM((NX, ROWS + 1, GROUP, COLS), F32),
-        pltpu.VMEM((NX, ROWS + 1, GROUP, COLS), F32),
-        pltpu.VMEM((NY, CPY, ROWS * GROUP), BF16),
-        pltpu.VMEM((NY, CPY, ROWS * GROUP), BF16),
+        pltpu.VMEM((NC * NX, TILTS, BAND + 1, GROUP, COLS), F32),
+        pltpu.VMEM((NX, TILTS, BAND + 1, GROUP, COLS), F32),
+        pltpu.VMEM((NX, TILTS, BAND + 1, GROUP, COLS), F32),
+        pltpu.VMEM((TILTS, NY, CPY, BAND * GROUP), BF16),
+        pltpu.VMEM((TILTS, NY, CPY, BAND * GROUP), BF16),
         pltpu.VMEM((ROWS * GROUP, CELLS), BF16),
         pltpu.VMEM((NZ, CPY, SLAB), BF16),
         pltpu.VMEM((NZ, CPY, SLAB), BF16),
@@ -452,8 +460,8 @@
         pltpu.VMEM((GROUP, COLS), F32),
         pltpu.VMEM((PARTS * ROWS, COLS), F32),
         pltpu.VMEM((PARTS, TILTS, BAND, COLS), BF16),
-        pltpu.SemaphoreType.DMA((LAST + NX,)),
-        pltpu.SemaphoreType.DMA((LAST + NX,)),
+        pltpu.SemaphoreType.DMA((EXCHANGES,)),
+        pltpu.SemaphoreType.DMA((EXCHANGES,)),
         pltpu.SemaphoreType.DMA((8,)),
     ]
     residual, warp_grad, back_volume = pl.pallas_call(

time: 70.4 us -> 64.7 us (0.919)
  Pallas kernels: 69.5 us -> 63.8 us
    pallas_call x1, Pallas kernels: 67.2 us -> 61.4 us  [shards(): pl.pallas_call(kernel, out_shape=(jax.ShapeDtypeStruct((PARTS, TILTS, BAN...]
where the time goes in v3:
time: 64.7 us; the launch traced here: 64.4 us
  Pallas kernels  63.8 us (99%)
    pallas_call x1, Pallas kernels, shards(): pl.pallas_call(kernel, out_shape=(jax.ShapeDtypeStruct((PARTS, TILTS, BAN...  61.4 us
    pallas_call x1, Pallas kernels, shards(): pl.pallas_call(hand_over, out_shape=(jax.ShapeDtypeStruct(residual.shape,...  2.37 us

profile of v3, /device:TPU:1, one launch (start us, length us, event | category | flops | bytes accessed | tf_op | source)
XLA Modules:
  0.0 64.4 jit_solution(1497101808008877692)
XLA Ops:
  0.6 61.4 %refine.1 = (bf16[256,3,8,128]{3,2,1,0:T(8,128)(2,1)}, f32[3,2,4]{2,1,0:T(2,128)}, f32[512,128]{1,0:T(8,128)}) custom-call(bf16[512,128]{1,0:T(8,128)(2,1)} %vol_in.1, s32[3,2,64]{2,1,0:T(2,128)} %bitcast.4, f32[3,2,64]{2,1,0:T(2,128)} %bitcast.5, bf16[3,2,4]{2,1,0:T(2,128)(2,1)} %bitcast.6, s32[256]{0:T(256)} %series_in.1, f32[256]{0:T(256)} %pos_in.1, ...), custom_call_target="tpu_custom_call" | custom-call | tf_op jit(solution)/shard_map/refine/pallas_call | solution.py:467
  62.1 2.4 %hand_over.1 = (bf16[256,3,8,128]{3,2,1,0:T(8,128)(2,1)}, f32[3,2,4]{2,1,0:T(2,128)}, f32[512,128]{1,0:T(8,128)}) custom-call(bf16[256,3,8,128]{3,2,1,0:T(8,128)(2,1)} %get-tuple-element.9.res_in, f32[3,2,4]{2,1,0:T(2,128)} %get-tuple-element.10.grad_in, f32[512,128]{1,0:T(8,128)} %get-tuple-element.11.back_in), custom_call_target="tpu_custom_call" | custom-call | tf_op jit(solution)/shard_map/hand_over/pallas_call | solution.py:490

commit v4 on v3

--- a/solution.py
+++ b/solution.py
@@ -19,8 +19,8 @@
 CELLS = BOX * BOX
 CPY = COLS // NY
 
-(META_Y, META_X, META_C, PZ, PY, PX, PC, VZ, VC, VX, VY, QC, QX, QY, QZ) = range(15)
-SC, SX, SY, EXCHANGES = 15, 15 + TILTS, 15 + 2 * TILTS, 15 + 3 * TILTS
+(META_Y, META_X, META_C, PZ, PY, PX, PC, VZ, VC, VX, VY, QC, QX, QY, QZ, PXY) = range(16)
+SC, SX, SY, EXCHANGES = 16, 16 + TILTS, 16 + 2 * TILTS, 16 + 3 * TILTS
 
 
 def split2(v):
@@ -110,7 +110,7 @@
 
     def send(row, axis, src, dst, bulk):
         size = {"y": NY, "x": NX, "c": NC, "z": NZ}[axis]
-        for k in range(1, size):
+        for k in sorted(range(1, size), key=lambda k: -min(k, size - k)):
             device, there = spot(axis, k)
             remote(row, device, src(there), dst).start()
         whole = remote(row, spot(axis, 1)[0], bulk, bulk)
@@ -122,7 +122,8 @@
     barrier = pltpu.get_barrier_semaphore()
     partners = [spot(axis, k)[0] for axis, size in (("c", NC), ("z", NZ)) for k in range(1, size)]
     plane = []
-    for j in range(1, NY * NX):
+    steps = [min(j // NX, NY - j // NX) + min(j % NX, NX - j % NX) for j in range(NY * NX)]
+    for j in sorted(range(1, NY * NX), key=lambda j: -steps[j]):
         there = lax.rem(y + j // NX, NY) * NX + lax.rem(x + j % NX, NX)
         plane.append((there * NC + c, z))
     for device in partners + plane:
@@ -244,18 +245,23 @@
 
     other, there = spot("c", 1)
     c_copies, s_x, s_y = [], [], []
+    squares = jnp.zeros((NS, COLS), F32)
+    for t in range(TILTS):
+        total = jnp.sum(jnp.where(hit, scale[t] * scale[t], 0.0), axis=1, keepdims=True)
+        squares = jnp.where(lane == t, total, squares)
+    bs[:, 0] = squares.reshape(NC * NX, GROUP, COLS)
+    slabs = [(0 if t == 0 else 1 + t * BAND, 1 + (t + 1) * BAND) for t in range(TILTS)]
     for t in range(TILTS):
         weight = jnp.where(hit, scale[t], 0.0)
-        squares = jnp.sum(weight * weight, axis=1, keepdims=True)
         both = jnp.concatenate(split2(weight), axis=0)
         for u in range(0, BAND, 2):
             r = t * BAND + u
             pair = dot(both, jnp.concatenate([xt[r], xt[r + 1]], axis=1))
             pair = pair[:NS] + pair[NS:]
-            bs[:, t, u] = pair[:, :COLS].reshape(NC * NX, GROUP, COLS)
-            bs[:, t, u + 1] = pair[:, COLS:].reshape(NC * NX, GROUP, COLS)
-        bs[:, t, BAND] = jnp.broadcast_to(squares, (NS, COLS)).reshape(NC * NX, GROUP, COLS)
-        c_copies.append(remote(SC + t, other, bs.at[pl.ds(there * NX, NX), t], brc.at[:, t]))
+            bs[:, 1 + r] = pair[:, :COLS].reshape(NC * NX, GROUP, COLS)
+            bs[:, 2 + r] = pair[:, COLS:].reshape(NC * NX, GROUP, COLS)
+        lo, hi = slabs[t]
+        c_copies.append(remote(SC + t, other, bs.at[pl.ds(there * NX, NX), lo:hi], brc.at[:, lo:hi]))
         c_copies[t].start()
 
     p_z.wait_recv()
@@ -263,20 +269,29 @@
     for k in range(1, NZ):
         own = own + prcv[lax.rem(z + k, NZ)]
     pall[c, x, y] = own.reshape(OWN * ROWS, COLS).astype(BF16)
+    p_x = send(PX, "x", lambda there: pall.at[c, x, y], pall.at[c, x, y], pall.at[0, 0, 0 : NX - 1])
     p_y = send(PY, "y", lambda there: pall.at[c, x, y], pall.at[c, x, y], pall.at[0, 0, 0 : NY - 1])
 
 
     for t in range(TILTS):
         c_copies[t].wait_recv()
-        brc[:, t] = brc[:, t] + bs[pl.ds(c * NX, NX), t]
-        bulk = brx.at[0 : NX - 1, t]
+        lo, hi = slabs[t]
+        brc[:, lo:hi] = brc[:, lo:hi] + bs[pl.ds(c * NX, NX), lo:hi]
+        bulk = brx.at[0 : NX - 1, lo:hi]
         s_x.append(
-            send(SX + t, "x", lambda there: brc.at[there, t], brx.at[x, t], bulk)
+            send(SX + t, "x", lambda there: brc.at[there, lo:hi], brx.at[x, lo:hi], bulk)
         )
     sent += c_copies
 
+    p_x.wait_recv()
+    for k in (4, 3, 5, 2, 6, 1, 7):
+        for j in range(1, NX):
+            block = pall.at[c, lax.rem(x + j, NX), y]
+            remote(PXY, spot("y", k)[0], block, block).start()
+    bulk = pall.at[0, 0 : NX - 1, 0 : NY - 1]
+    p_xy = remote(PXY, other, bulk, bulk)
+    sent.append(p_xy)
     p_y.wait_recv()
-    p_x = send(PX, "x", lambda there: pall.at[c, x], pall.at[c, x], pall.at[0, 0 : NX - 1])
     pgf[...] = pall[c, x].reshape(GROUP * ROWS, COLS).astype(F32)
 
     flat_group = meta.at[c, pl.ds(x * NY, NY)].reshape(NY * 8, COLS)
@@ -293,13 +308,16 @@
 
     for t in range(TILTS):
         s_x[t].wait_recv()
-        total = brc[x, t]
+        lo, hi = slabs[t]
+        total = brc[x, lo:hi]
         for k in range(1, NX):
-            total = total + brx[lax.rem(x + k, NX), t]
+            total = total + brx[lax.rem(x + k, NX), lo:hi]
+        if t == 0:
+            squares, total = total[0], total[1:]
         fixed = []
         for u in range(BAND):
             guess = pgf[pl.ds(t * BAND + u, GROUP, stride=ROWS), :]
-            fixed.append(total[u] - total[BAND] * guess)
+            fixed.append(total[u] - squares[:, t : t + 1] * guess)
         turned = jnp.transpose(jnp.concatenate(fixed, axis=0))
         ysrc[t] = turned.reshape(NY, CPY, BAND * GROUP).astype(BF16)
         bulk = yrcv.at[t, 0 : NY - 1]
@@ -312,7 +330,7 @@
     factors = jnp.transpose(jnp.concatenate(scale + basis + [basis[0]], axis=0))
     inner = jnp.zeros((PARTS, COLS), F32)
 
-    p_x.wait_recv()
+    p_xy.wait_recv()
     p_c = send(PC, "c", lambda there: pall.at[c], pall.at[c], pall.at[0])
     totals = []
     for t in range(TILTS):
@@ -372,7 +390,7 @@
     crcv[c] = total
     v_c = send(VC, "c", lambda there: crcv.at[c], crcv.at[c], crcv.at[0])
     v_c.wait_recv()
-    xrcv[x] = crcv[0] + crcv[1]
+    xrcv[x] = (crcv[0] + crcv[1]).astype(BF16)
     v_x = send(VX, "x", lambda there: xrcv.at[x], xrcv.at[x], xrcv.at[0 : NX - 1])
     q_x.wait_recv()
     total = qrc[x]
@@ -381,7 +399,8 @@
     qry[y] = total
     q_y = send(QY, "y", lambda there: qry.at[y], qry.at[y], qry.at[0 : NY - 1])
     v_x.wait_recv()
-    vall[y] = ((xrcv[0] + xrcv[1]) + (xrcv[2] + xrcv[3])).astype(BF16)
+    rows = [xrcv[k].astype(F32) for k in range(NX)]
+    vall[y] = ((rows[0] + rows[1]) + (rows[2] + rows[3])).astype(BF16)
     v_y = send(VY, "y", lambda there: vall.at[y], vall.at[y], vall.at[0 : NY - 1])
     q_y.wait_recv()
     total = qry[0]
@@ -441,16 +460,16 @@
         pltpu.VMEM((NC, NX, NY, OWN * ROWS, COLS), BF16),
         pltpu.VMEM((GROUP * ROWS, COLS), F32),
         pltpu.VMEM((NS * ROWS, COLS), F32),
-        pltpu.VMEM((NC * NX, TILTS, BAND + 1, GROUP, COLS), F32),
-        pltpu.VMEM((NX, TILTS, BAND + 1, GROUP, COLS), F32),
-        pltpu.VMEM((NX, TILTS, BAND + 1, GROUP, COLS), F32),
+        pltpu.VMEM((NC * NX, 1 + ROWS, GROUP, COLS), F32),
+        pltpu.VMEM((NX, 1 + ROWS, GROUP, COLS), F32),
+        pltpu.VMEM((NX, 1 + ROWS, GROUP, COLS), F32),
         pltpu.VMEM((TILTS, NY, CPY, BAND * GROUP), BF16),
         pltpu.VMEM((TILTS, NY, CPY, BAND * GROUP), BF16),
         pltpu.VMEM((ROWS * GROUP, CELLS), BF16),
         pltpu.VMEM((NZ, CPY, SLAB), BF16),
         pltpu.VMEM((NZ, CPY, SLAB), BF16),
         pltpu.VMEM((NC, CPY, SLAB), F32),
-        pltpu.VMEM((NX, CPY, SLAB), F32),
+        pltpu.VMEM((NX, CPY, SLAB), BF16),
         pltpu.VMEM((NY, CPY, SLAB), BF16),
         pltpu.VMEM((NC, NX, GROUP, COLS), F32),
         pltpu.VMEM((NX, GROUP, COLS), F32),

time: 64.7 us -> 60.8 us (0.940)
  Pallas kernels: 63.8 us -> 59.9 us
    pallas_call x1, Pallas kernels: 61.4 us -> 57.5 us  [shards(): pl.pallas_call(kernel, out_shape=(jax.ShapeDtypeStruct((PARTS, TILTS, BAN...]
where the time goes in v4:
time: 60.8 us; the launch traced here: 60.5 us
  Pallas kernels  59.9 us (99%)
  between operations  0.64 us (1%)
    pallas_call x1, Pallas kernels, shards(): pl.pallas_call(kernel, out_shape=(jax.ShapeDtypeStruct((PARTS, TILTS, BAN...  57.5 us
    pallas_call x1, Pallas kernels, shards(): pl.pallas_call(hand_over, out_shape=(jax.ShapeDtypeStruct(residual.shape,...  2.37 us

profile of v4, /device:TPU:1, one launch (start us, length us, event | category | flops | bytes accessed | tf_op | source)
XLA Modules:
  0.0 60.5 jit_solution(17680322703296277238)
XLA Ops:
  0.6 57.5 %refine.1 = (bf16[256,3,8,128]{3,2,1,0:T(8,128)(2,1)}, f32[3,2,4]{2,1,0:T(2,128)}, f32[512,128]{1,0:T(8,128)}) custom-call(bf16[512,128]{1,0:T(8,128)(2,1)} %vol_in.1, s32[3,2,64]{2,1,0:T(2,128)} %bitcast.4, f32[3,2,64]{2,1,0:T(2,128)} %bitcast.5, bf16[3,2,4]{2,1,0:T(2,128)(2,1)} %bitcast.6, s32[256]{0:T(256)} %series_in.1, f32[256]{0:T(256)} %pos_in.1, ...), custom_call_target="tpu_custom_call" | custom-call | tf_op jit(solution)/shard_map/refine/pallas_call | solution.py:486
  58.2 2.4 %hand_over.1 = (bf16[256,3,8,128]{3,2,1,0:T(8,128)(2,1)}, f32[3,2,4]{2,1,0:T(2,128)}, f32[512,128]{1,0:T(8,128)}) custom-call(bf16[256,3,8,128]{3,2,1,0:T(8,128)(2,1)} %get-tuple-element.9.res_in, f32[3,2,4]{2,1,0:T(2,128)} %get-tuple-element.10.grad_in, f32[512,128]{1,0:T(8,128)} %get-tuple-element.11.back_in), custom_call_target="tpu_custom_call" | custom-call | tf_op jit(solution)/shard_map/hand_over/pallas_call | solution.py:509

commit v5 on v4

--- a/solution.py
+++ b/solution.py
@@ -74,11 +74,9 @@
     wsp,
     zsrc,
     zrcv,
-    crcv,
     xrcv,
     vall,
     qsrc,
-    qrc,
     qrx,
     qry,
     qrz,
@@ -117,16 +115,25 @@
         sent.append(whole)
         return whole
 
+    def send_group(row, src, dst, bulk):
+        for k in (2, 6, 1, 3, 5, 7, 4):
+            xx, cc = lax.rem(x + k % NX, NX), lax.rem(c + k // NX, NC)
+            remote(row, ((y * NX + xx) * NC + cc, z), src(cc, xx), dst).start()
+        whole = remote(row, spot("c", 1)[0], bulk, bulk)
+        sent.append(whole)
+        return whole
+
     sent = []
 
     barrier = pltpu.get_barrier_semaphore()
-    partners = [spot(axis, k)[0] for axis, size in (("c", NC), ("z", NZ)) for k in range(1, size)]
+    partners = [spot("z", k)[0] for k in range(1, NZ)]
+    partners += [((y * NX + lax.rem(x + k, NX)) * NC + 1 - c, z) for k in range(NX)]
     plane = []
     steps = [min(j // NX, NY - j // NX) + min(j % NX, NX - j % NX) for j in range(NY * NX)]
     for j in sorted(range(1, NY * NX), key=lambda j: -steps[j]):
         there = lax.rem(y + j // NX, NY) * NX + lax.rem(x + j % NX, NX)
         plane.append((there * NC + c, z))
-    for device in partners + plane:
+    for device in plane + partners:
         pl.semaphore_signal(barrier, inc=1, device_id=device, device_id_type=MESH)
 
     small_copies = [
@@ -341,10 +348,14 @@
         totals.append(total)
     total = jnp.concatenate(totals, axis=1)
     both = jnp.concatenate(split2(total), axis=0)
-    for k in range(NZ):
-        part = dot(both, wsp[:, k * SLAB : (k + 1) * SLAB])
-        zsrc[k] = (part[:CPY] + part[CPY:]).astype(BF16)
-    v_z = send(VZ, "z", lambda there: zsrc.at[there], zrcv.at[z], zrcv.at[0 : NZ - 1])
+    for k in (4, 3, 5, 2, 6, 1, 7, 0):
+        device, at = spot("z", k)
+        part = dot(both, wsp[:, pl.ds(pl.multiple_of(at * SLAB, SLAB), SLAB)])
+        zsrc[at] = (part[:CPY] + part[CPY:]).astype(BF16)
+        if k > 0:
+            remote(VZ, device, zsrc.at[at], zrcv.at[z]).start()
+    v_z = remote(VZ, other, zrcv.at[1:], zrcv.at[1:])
+    sent.append(v_z)
 
     p_c.wait_recv()
     pf[...] = pall[...].reshape(NS * ROWS, COLS).astype(F32)
@@ -362,45 +373,42 @@
                 acc = acc + left * guess
         inner = jnp.where(lane_p // CTRL == t, jnp.sum(acc, axis=1, keepdims=True), inner)
 
-    def narrow(i, _):
-        for k in range(16):
-            part = rf[pl.ds(i * 16 + k, ROWS, stride=PARTS), :]
-            rb[i * 16 + k] = part.reshape(TILTS, BAND, COLS).astype(BF16)
-        return 0
-
-    lax.fori_loop(0, PARTS // 16, narrow, 0)
-    for k in range(8):
-        rows = pl.ds(k * step, step)
-        pltpu.make_async_copy(rb.at[rows], res_out.at[rows], lsem.at[7]).start()
     term = jnp.zeros((PARTS, COLS), F32)
     for k in range(CTRL):
         term = jnp.where(lax.rem(lane_p, CTRL) == k, factors[:, TILTS + k : TILTS + k + 1] * inner, term)
     hi, mid, lo = split3(term)
     grad = (dot(hot16, hi) + (dot(hot16, mid) + dot(hot16, lo))) * (-1.0 / (BOX * BOX))
     qsrc[...] = grad.reshape(NC, NX, GROUP, COLS)
-    q_c = send(QC, "c", lambda there: qsrc.at[there], qrc, qrc)
-
-    q_c.wait_recv()
-    qrc[...] = qrc[...] + qsrc[c]
-    q_x = send(QX, "x", lambda there: qrc.at[there], qrx.at[x], qrx.at[0 : NX - 1])
+    q_x = send_group(QX, lambda cc, xx: qsrc.at[cc, xx], qrx.at[c * NX + x], qrx.at[1:])
+
+    def narrow(i, _):
+        for k in range(16):
+            part = rf[pl.ds(i * 16 + k, ROWS, stride=PARTS), :]
+            rb[i * 16 + k] = part.reshape(TILTS, BAND, COLS).astype(BF16)
+        return 0
+
+    lax.fori_loop(0, PARTS // 16, narrow, 0)
+    for k in range(8):
+        rows = pl.ds(k * step, step)
+        pltpu.make_async_copy(rb.at[rows], res_out.at[rows], lsem.at[7]).start()
     v_z.wait_recv()
     total = zsrc[z].astype(F32)
     for k in range(1, NZ):
         total = total + zrcv[lax.rem(z + k, NZ)].astype(F32)
-    crcv[c] = total
-    v_c = send(VC, "c", lambda there: crcv.at[c], crcv.at[c], crcv.at[0])
-    v_c.wait_recv()
-    xrcv[x] = (crcv[0] + crcv[1]).astype(BF16)
-    v_x = send(VX, "x", lambda there: xrcv.at[x], xrcv.at[x], xrcv.at[0 : NX - 1])
+    at_group = c * NX + x
+    xrcv[at_group] = total.astype(BF16)
+    v_x = send_group(VX, lambda cc, xx: xrcv.at[at_group], xrcv.at[at_group], xrcv.at[1:])
     q_x.wait_recv()
-    total = qrc[x]
-    for k in range(1, NX):
-        total = total + qrx[lax.rem(x + k, NX)]
+    total = qsrc[c, x]
+    for k in range(1, NC * NX):
+        total = total + qrx[lax.rem(c + k // NX, NC) * NX + lax.rem(x + k, NX)]
     qry[y] = total
     q_y = send(QY, "y", lambda there: qry.at[y], qry.at[y], qry.at[0 : NY - 1])
     v_x.wait_recv()
-    rows = [xrcv[k].astype(F32) for k in range(NX)]
-    vall[y] = ((rows[0] + rows[1]) + (rows[2] + rows[3])).astype(BF16)
+    total = xrcv[0].astype(F32)
+    for k in range(1, NC * NX):
+        total = total + xrcv[k].astype(F32)
+    vall[y] = total.astype(BF16)
     v_y = send(VY, "y", lambda there: vall.at[y], vall.at[y], vall.at[0 : NY - 1])
     q_y.wait_recv()
     total = qry[0]
@@ -468,12 +476,10 @@
         pltpu.VMEM((ROWS * GROUP, CELLS), BF16),
         pltpu.VMEM((NZ, CPY, SLAB), BF16),
         pltpu.VMEM((NZ, CPY, SLAB), BF16),
-        pltpu.VMEM((NC, CPY, SLAB), F32),
-        pltpu.VMEM((NX, CPY, SLAB), BF16),
+        pltpu.VMEM((NC * NX, CPY, SLAB), BF16),
         pltpu.VMEM((NY, CPY, SLAB), BF16),
         pltpu.VMEM((NC, NX, GROUP, COLS), F32),
-        pltpu.VMEM((NX, GROUP, COLS), F32),
-        pltpu.VMEM((NX, GROUP, COLS), F32),
+        pltpu.VMEM((NC * NX, GROUP, COLS), F32),
         pltpu.VMEM((NY, GROUP, COLS), F32),
         pltpu.VMEM((NZ, GROUP, COLS), F32),
         pltpu.VMEM((GROUP, COLS), F32),

time: 60.8 us -> 60.1 us (0.988)
  Pallas kernels: 59.9 us -> 59.2 us
    pallas_call x1, Pallas kernels: 57.5 us -> 56.9 us  [shards(): pl.pallas_call(kernel, out_shape=(jax.ShapeDtypeStruct((PARTS, TILTS, BAN...]
where the time goes in v5:
time: 60.1 us; the launch traced here: 59.9 us
  Pallas kernels  59.2 us (99%)
  between operations  0.64 us (1%)
    pallas_call x1, Pallas kernels, shards(): pl.pallas_call(kernel, out_shape=(jax.ShapeDtypeStruct((PARTS, TILTS, BAN...  56.9 us
    pallas_call x1, Pallas kernels, shards(): pl.pallas_call(hand_over, out_shape=(jax.ShapeDtypeStruct(residual.shape,...  2.37 us

profile of v5, /device:TPU:1, one launch (start us, length us, event | category | flops | bytes accessed | tf_op | source)
XLA Modules:
  0.0 59.9 jit_solution(9571545107591644937)
XLA Ops:
  0.6 56.9 %refine.1 = (bf16[256,3,8,128]{3,2,1,0:T(8,128)(2,1)}, f32[3,2,4]{2,1,0:T(2,128)}, f32[512,128]{1,0:T(8,128)}) custom-call(bf16[512,128]{1,0:T(8,128)(2,1)} %vol_in.1, s32[3,2,64]{2,1,0:T(2,128)} %bitcast.4, f32[3,2,64]{2,1,0:T(2,128)} %bitcast.5, bf16[3,2,4]{2,1,0:T(2,128)(2,1)} %bitcast.6, s32[256]{0:T(256)} %series_in.1, f32[256]{0:T(256)} %pos_in.1, ...), custom_call_target="tpu_custom_call" | custom-call | tf_op jit(solution)/shard_map/refine/pallas_call | solution.py:492
  57.5 2.4 %hand_over.1 = (bf16[256,3,8,128]{3,2,1,0:T(8,128)(2,1)}, f32[3,2,4]{2,1,0:T(2,128)}, f32[512,128]{1,0:T(8,128)}) custom-call(bf16[256,3,8,128]{3,2,1,0:T(8,128)(2,1)} %get-tuple-element.9.res_in, f32[3,2,4]{2,1,0:T(2,128)} %get-tuple-element.10.grad_in, f32[512,128]{1,0:T(8,128)} %get-tuple-element.11.back_in), custom_call_target="tpu_custom_call" | custom-call | tf_op jit(solution)/shard_map/hand_over/pallas_call | solution.py:515
